TPU v7x, 512 devices: a whole 4x8x8 slice. The times are simulated.
512 devices in a mesh: chan: 16 (over y, core), space: 8 (over z), sample: 4 (over x).
Axes of the slice: x: 4, y: 8, z: 8, core: 2. Of those that a mesh axis runs over, the one named last changes fastest.
Arguments:
- inputs: bfloat16 [4, 128, 16, 4096], P('sample', 'chan', 'space'), may hold values from -6 to 6
- weights: bfloat16 [27, 128, 128], P(None, 'chan'), may hold values from -0.125 to 0.125
- grad_out: bfloat16 [4, 128, 16, 4096], P('sample', 'chan', 'space'), may hold values from -6 to 6
Outputs:
- output: bfloat16 [4, 128, 16, 4096], P('sample', 'chan', 'space')
- grad_in: bfloat16 [4, 128, 16, 4096], P('sample', 'chan', 'space')
- grad_weights: float32 [27, 128, 128], P(None, 'chan')
All inputs are finite; a program needn't handle non-finite values.
Results may differ from a plain program's by a relative error of at most 0.001.
Values may be sent and summed in bfloat16 or wider, within the bound.
No kernel may reach another device: no remote copies, remote signals or barrier semaphores. Data moves between devices by JAX's collectives and lax.ppermute only.
A program may use at most 64 MiB of HBM per device.

v0:
```python
import math

import jax
import jax.numpy as jnp
from jax import lax
from jax.sharding import PartitionSpec as P

SIDE = 64


def extended(block, sides, width):
    for axis, dim in sides:
        count = lax.axis_size(axis)
        forward = [(i, i + 1) for i in range(count - 1)]
        backward = [(target, source) for source, target in forward]
        low = lax.ppermute(
            lax.slice_in_dim(block, block.shape[dim] - width, None, axis=dim), axis, forward
        )
        high = lax.ppermute(lax.slice_in_dim(block, 0, width, axis=dim), axis, backward)
        block = jnp.concatenate([low, block, high], axis=dim)
    return block


def shift_plane(block, row_shift, col_shift):
    cells = block.shape[-1]
    margin = SIDE + 1
    widths = [(0, 0)] * (block.ndim - 1) + [(margin, margin)]
    padded = jnp.pad(block, widths)
    first_cell = margin + row_shift * SIDE + col_shift
    moved = lax.slice_in_dim(padded, first_cell, first_cell + cells, axis=block.ndim - 1)
    column = jnp.arange(cells) % SIDE + col_shift
    inside = (column >= 0) & (column < SIDE)
    return jnp.where(inside, moved, jnp.zeros((), block.dtype))


def unfold(padded_x, planes):
    pieces = []
    for plane_k in range(3):
        depth_slab = padded_x[:, plane_k : plane_k + planes, :]
        for row_k in range(3):
            for col_k in range(3):
                pieces.append(shift_plane(depth_slab, row_k - 1, col_k - 1))
    stacked = jnp.stack(pieces, 0)
    return stacked.reshape(stacked.shape[0] * stacked.shape[1], planes * stacked.shape[3])


def local(inputs, weights, grad_out):
    c_dev = inputs.shape[1]
    planes = inputs.shape[2]
    cells = inputs.shape[3]
    out_all = weights.shape[2]
    o_dev = grad_out.shape[1]
    padded = extended(inputs[0], (("space", 1),), 1)
    columns_x = unfold(padded, planes)
    flat_weights = weights.reshape(27 * c_dev, out_all)
    partial_product = lax.dot_general(
        flat_weights, columns_x, (((0,), (0,)), ((), ())), preferred_element_type=jnp.float32
    )
    output = lax.psum_scatter(
        partial_product.reshape(o_dev * lax.axis_size("chan"), planes, cells),
        "chan",
        scatter_dimension=0,
        tiled=True,
    ).astype(jnp.bfloat16)
    with_rims = extended(grad_out[0], (("space", 1),), 1)
    grad_all = lax.all_gather(with_rims, "chan", axis=0, tiled=True)
    kernel_rows = weights.reshape(3, 9 * c_dev, out_all)
    grad_sum = jnp.zeros((c_dev, planes, cells), jnp.float32)
    for plane_k in range(3):
        depth_slab = grad_all[:, 2 - plane_k : 2 - plane_k + planes, :].reshape(
            out_all, planes * cells
        )
        product = jnp.dot(kernel_rows[plane_k], depth_slab, preferred_element_type=jnp.float32)
        product = product.reshape(9, c_dev, planes, cells)
        for position in range(9):
            row_k = position // 3
            col_k = position % 3
            grad_sum = grad_sum + shift_plane(product[position], 1 - row_k, 1 - col_k)
    interior = grad_all[:, 1 : 1 + planes, :].reshape(out_all, planes * cells)
    local_grads = lax.dot_general(
        columns_x, interior, (((1,), (1,)), ((), ())), preferred_element_type=jnp.float32
    )
    local_grads = local_grads.reshape(27, c_dev, out_all)
    grad_scale = 1.0 / math.sqrt(lax.axis_size("space") * lax.axis_size("sample") * planes * cells)
    grad_weights = lax.psum(local_grads * grad_scale, ("space", "sample"))
    return (output[None], grad_sum.astype(jnp.bfloat16)[None], grad_weights)


def solution(mesh):
    in_specs = (
        P("sample", "chan", "space", None),
        P(None, "chan", None),
        P("sample", "chan", "space", None),
    )
    out_specs = (
        P("sample", "chan", "space", None),
        P("sample", "chan", "space", None),
        P(None, "chan", None),
    )
    return jax.shard_map(local, mesh=mesh, in_specs=in_specs, out_specs=out_specs, check_vma=False)
```

profile of v0, /device:TPU:1, one launch (start us, length us, event | category | flops | bytes accessed | tf_op | source)
XLA Modules:
  0.0 285.3 jit_solution(6294775749122549562)
XLA Ops:
  7.2 1.0 copy.32
  8.2 1.3 collective-permute-start.1
  9.5 5.5 %collective-permute-start = (bf16[8,1,4096]{2,0,1:T(8,128)(2,1)S(1)}, bf16[8,1,4096]{2,0,1:T(8,128)(2,1)S(1)}, u32[]{:S(2)}, u32[]{:S(2)}) collective-permute-start(bf16[8,1,4096]{2,0,1:T(8,128)(2,1)S(1)} %get-tuple-element.47), channel_id=1, source_target_pairs={{0,4},{4,8},{8,12},{12,16},{16,20},{20,24},{24,28},{1,5},{5,9},{9,... | collective-permute-start | bytes 196616 | tf_op jit(solution)/shard_map/ppermute | solution.py:16
  15.0 1.0 copy.31
  16.0 4.0 %collective-permute-start.2 = (bf16[8,1,4096]{2,0,1:T(8,128)(2,1)S(1)}, bf16[8,1,4096]{2,0,1:T(8,128)(2,1)S(1)}, u32[]{:S(2)}, u32[]{:S(2)}) collective-permute-start(bf16[8,1,4096]{2,0,1:T(8,128)(2,1)S(1)} %get-tuple-element.42), channel_id=1, source_target_pairs={{0,4},{4,8},{8,12},{12,16},{16,20},{20,24},{24,28},{1,5},{5,9},{9,... | collective-permute-start | bytes 196616 | tf_op jit(solution)/shard_map/ppermute | solution.py:16
  20.0 1.3 collective-permute-start.3
  21.3 1.3 dynamic-slice
  23.3 2.4 collective-permute-done.3
  25.7 0.8 pad_maximum_fusion
  26.7 0.1 bitcast_dynamic-update-slice_fusion.24
  26.8 0.1 bitcast_dynamic-update-slice_fusion.23
  26.9 0.1 bitcast_dynamic-update-slice_fusion.22
  27.1 0.1 bitcast_dynamic-update-slice_fusion.20
  27.2 0.1 bitcast_dynamic-update-slice_fusion.19
  27.3 0.1 bitcast_dynamic-update-slice_fusion.18
  27.4 0.1 bitcast_dynamic-update-slice_fusion.17
  27.5 1.0 bitcast_dynamic-update-slice_fusion.16
  28.5 1.0 bitcast_dynamic-update-slice_fusion.15
  29.5 1.0 bitcast_dynamic-update-slice_fusion.14
  30.6 1.0 bitcast_dynamic-update-slice_fusion.13
  31.7 0.1 bitcast_dynamic-update-slice_fusion.12
  31.8 0.1 bitcast_dynamic-update-slice_fusion.11
  31.9 0.1 bitcast_dynamic-update-slice_fusion.10
  32.0 0.1 bitcast_dynamic-update-slice_fusion.9
  32.1 0.1 bitcast_dynamic-update-slice_fusion.8
  32.3 0.1 bitcast_dynamic-update-slice_fusion.7
  32.4 0.1 bitcast_dynamic-update-slice_fusion.6
  32.5 0.1 bitcast_dynamic-update-slice_fusion.5
  33.1 3.4 %fusion.61 = f32[8192,128]{1,0:T(8,128)} fusion(bf16[216,8192]{1,0:T(8,128)(2,1)S(1)} %bitcast.132, bf16[27,8,128]{2,1,0:T(8,128)(2,1)S(1)} %copy-done.16), kind=kOutput, calls=%fused_computation.117 | convolution fusion | flops 452984832 | bytes 7788544 | tf_op jit(solution)/shard_map/dot_general | solution.py:56
  36.5 7.3 %copy.21 = f32[128,2,4096]{2,1,0:T(2,128)} copy(f32[128,2,4096]{0,2,1:T(8,128)} %bitcast.133) | data formatting | bytes 8388608 | tf_op jit(solution)/shard_map/reshape | solution.py:60
  43.8 78.6 %all-reduce.32 = bf16[128,2,4096]{2,1,0:T(2,128)(2,1)} all-reduce(f32[128,2,4096]{2,1,0:T(2,128)} %copy.21), channel_id=2, replica_groups=mesh['chan'=16,'space'=8,'sample'=4] {'chan'}, use_global_device_ids=true, to_apply=%region_0.1.clone | all-reduce | flops 1048576 | bytes 6291456
  122.4 1.7 fusion.59
  124.0 3.3 %fusion.5 = f32[27,8,128]{2,1,0:T(8,128)} fusion(bf16[27,8,2,4096]{3,1,2,0:T(8,128)(2,1)S(1)} %bitcast_dynamic-update-slice_fusion, bf16[128,4,4096]{2,0,1:T(8,128)(2,1)} %all-gather.2.cloned.1.call-done), kind=kOutput, calls=%fused_computation.6 | convolution fusion | flops 453012480 | bytes 5746688 | tf_op jit(solution)/shard_map/dot_general | solution.py:80
  127.4 5.9 %fusion.84 = (bf16[128,2,4096]{2,0,1:T(8,128)(2,1)}, bf16[128,2,4096]{2,0,1:T(8,128)(2,1)}, bf16[128,2,4096]{2,0,1:T(8,128)(2,1)}) fusion(bf16[128,4,4096]{2,0,1:T(8,128)(2,1)} %all-gather.2.cloned.1.call-done), kind=kLoop, calls=%fused_computation.142 | loop fusion | bytes 12582912 | tf_op jit(solution)/shard_map/slice | solution.py:70
  133.2 3.1 %copy.23 = bf16[128,2,4096]{0,2,1:T(8,128)(2,1)S(1)} copy(bf16[128,2,4096]{2,0,1:T(8,128)(2,1)} %get-tuple-element.12) | data formatting | bytes 4194304 | tf_op jit(solution)/shard_map/slice | solution.py:70
  136.4 1.4 convolution_bitcast_fusion.2
  137.8 1.1 fusion.85
  138.9 3.1 %copy.25 = bf16[128,2,4096]{0,2,1:T(8,128)(2,1)S(1)} copy(bf16[128,2,4096]{2,0,1:T(8,128)(2,1)} %get-tuple-element.13) | data formatting | bytes 4194304 | tf_op jit(solution)/shard_map/slice | solution.py:70
  142.0 1.4 convolution_bitcast_fusion
  143.4 1.5 fusion.87
  144.8 3.1 %copy.24 = bf16[128,2,4096]{0,2,1:T(8,128)(2,1)S(1)} copy(bf16[128,2,4096]{2,0,1:T(8,128)(2,1)} %get-tuple-element.14) | data formatting | bytes 4194304 | tf_op jit(solution)/shard_map/slice | solution.py:70
  148.0 1.4 convolution_bitcast_fusion.1
  149.5 0.2 fusion.86
  149.7 0.7 copy-done.2
  151.3 1.7 fusion.60
  153.0 0.8 copy.26
  153.8 123.1 %all-reduce.31.cloned.1.call-done = f32[27,8,128]{2,1,0:T(8,128)} async-done(((f32[27,8,128]{2,1,0:T(8,128)}), f32[27,8,128]{2,1,0:T(8,128)}) %all-reduce.31.cloned.1.call-update) | async-done | bytes 110608 | tf_op jit(solution)/shard_map/psum | solution.py:85
  276.9 1.5 copy.62
  (56 shorter events, 1.9 us)
Async XLA Ops:
  7.2 116.9 %all-gather.2.cloned.1.call-start = ((), (), s32[]{:S(2)}) async-start(), calls=%async_computation | async-start | bytes 4456448 | tf_op jit(solution)/shard_map/all_gather | solution.py:66
  8.2 18.4 %copy-start = (bf16[1,8,2,4096]{3,1,2,0:T(8,128)(2,1)}, bf16[1,8,2,4096]{3,1,2,0:T(8,128)(2,1)S(1)}, u32[]{:S(2)}) copy-start(bf16[1,8,2,4096]{3,1,2,0:T(8,128)(2,1)S(1)} %copy.32) | copy-start | bytes 393220
  8.2 18.3 %collective-permute-start.1 = (bf16[8,1,4096]{2,0,1:T(8,128)(2,1)S(1)}, bf16[8,1,4096]{2,0,1:T(8,128)(2,1)S(1)}, u32[]{:S(2)}, u32[]{:S(2)}) collective-permute-start(bf16[8,1,4096]{2,0,1:T(8,128)(2,1)S(1)} %get-tuple-element.46), channel_id=1, source_target_pairs={{4,0},{8,4},{12,8},{16,12},{20,16},{24,20},{28,24},{5,1},{9,5},{13... | collective-permute-start | bytes 196616 | tf_op jit(solution)/shard_map/ppermute | solution.py:19
  9.5 17.0 %collective-permute-start = (bf16[8,1,4096]{2,0,1:T(8,128)(2,1)S(1)}, bf16[8,1,4096]{2,0,1:T(8,128)(2,1)S(1)}, u32[]{:S(2)}, u32[]{:S(2)}) collective-permute-start(bf16[8,1,4096]{2,0,1:T(8,128)(2,1)S(1)} %get-tuple-element.47), channel_id=1, source_target_pairs={{0,4},{4,8},{8,12},{12,16},{16,20},{20,24},{24,28},{1,5},{5,9},{9,... | collective-permute-start | bytes 196616 | tf_op jit(solution)/shard_map/ppermute | solution.py:16
  16.0 7.3 %collective-permute-start.2 = (bf16[8,1,4096]{2,0,1:T(8,128)(2,1)S(1)}, bf16[8,1,4096]{2,0,1:T(8,128)(2,1)S(1)}, u32[]{:S(2)}, u32[]{:S(2)}) collective-permute-start(bf16[8,1,4096]{2,0,1:T(8,128)(2,1)S(1)} %get-tuple-element.42), channel_id=1, source_target_pairs={{0,4},{4,8},{8,12},{12,16},{16,20},{20,24},{24,28},{1,5},{5,9},{9,... | collective-permute-start | bytes 196616 | tf_op jit(solution)/shard_map/ppermute | solution.py:16
  20.0 5.6 %collective-permute-start.3 = (bf16[8,1,4096]{2,0,1:T(8,128)(2,1)S(1)}, bf16[8,1,4096]{2,0,1:T(8,128)(2,1)S(1)}, u32[]{:S(2)}, u32[]{:S(2)}) collective-permute-start(bf16[8,1,4096]{2,0,1:T(8,128)(2,1)S(1)} %get-tuple-element.43), channel_id=1, source_target_pairs={{4,0},{8,4},{12,8},{16,12},{20,16},{24,20},{28,24},{5,1},{9,5},{13... | collective-permute-start | bytes 196616 | tf_op jit(solution)/shard_map/ppermute | solution.py:19
  26.4 250.5 %all-reduce.31.cloned.1.call-start = ((), (), s32[]{:S(2)}) async-start(), calls=%async_computation.1 | async-start | bytes 221184 | tf_op jit(solution)/shard_map/psum | solution.py:85
  26.5 5.1 %copy-start.15 = (bf16[1,8,2,4096]{3,2,1,0:T(2,128)(2,1)S(1)}, bf16[1,8,2,4096]{3,2,1,0:T(2,128)(2,1)}, u32[]{:S(2)}) copy-start(bf16[1,8,2,4096]{3,2,1,0:T(2,128)(2,1)} %param.3) | copy-start | bytes 393220
  26.6 5.1 %copy-start.1 = (bf16[1,8,2,4096]{3,1,2,0:T(8,128)(2,1)S(1)}, bf16[1,8,2,4096]{3,1,2,0:T(8,128)(2,1)}, u32[]{:S(2)}) copy-start(bf16[1,8,2,4096]{3,1,2,0:T(8,128)(2,1)} %copy-done) | copy-start | bytes 393220
  26.6 6.5 %copy-start.16 = (bf16[27,8,128]{2,1,0:T(8,128)(2,1)S(1)}, bf16[27,8,128]{2,1,0:T(8,128)(2,1)}, u32[]{:S(2)}) copy-start(bf16[27,8,128]{2,1,0:T(8,128)(2,1)} %param.4) | copy-start | bytes 165892
  133.2 3.1 %copy-start.17 = (bf16[27,8,128]{2,1,0:T(8,128)(2,1)S(1)}, bf16[27,8,128]{2,1,0:T(8,128)(2,1)}, u32[]{:S(2)}) copy-start(bf16[27,8,128]{2,1,0:T(8,128)(2,1)} %param.4) | copy-start | bytes 165892
  149.4 1.0 copy-start.2
  149.4 1.0 copy-start.3
  149.4 1.1 copy-start.4
  149.4 1.2 copy-start.5
  149.4 1.2 copy-start.6
  149.4 1.3 copy-start.7
  149.4 1.4 copy-start.8
  149.4 1.5 copy-start.9
  149.4 1.5 copy-start.10
  149.4 1.6 copy-start.11
  149.5 1.7 copy-start.12
  149.5 1.7 copy-start.13
  149.5 1.8 copy-start.14
Sparse Core Ops, SparseCore 0:
  26.5 52.9 all-gather.1
  127.5 149.3 all-reduce.30
where the time goes:
time: 289 us; the launch traced here: 285 us
  waiting for transfers between devices  126 us (44%)
  blocking collectives  78.6 us (27%)
  local copies, waits for them, and re-layouts  34.2 us (12%)
  between operations  15.2 us (5%)
  starting transfers between devices  12.1 us (4%)
  matrix products  10.8 us (4%)
  other arithmetic  8.8 us (3%)
    psum x1, waiting for transfers between devices, local(): grad_weights = lax.psum(local_grads * grad_scale, ('space', 'sample'))  123 us
    unnamed x1, blocking collectives  78.6 us
    slice x4, local copies, waits for them, and re-layouts, local(): grad_all[:, 2 - plane_k:2 - plane_k + planes, :]  15.3 us
    ppermute x2, starting transfers between devices, extended(): lax.ppermute(lax.slice_in_dim(block, block.shape[dim] - width, None, axis...  9.46 us
    reshape x1, local copies, waits for them, and re-layouts, local(): partial_product.reshape(o_dev * lax.axis_size('chan'), planes, cells)  7.33 us
    unnamed x41, local copies, waits for them, and re-layouts  7.25 us
    unnamed x26, other arithmetic  6.19 us
  transfers between devices with their start and end apart: 6, of which 2 were waited for; matrix products, arithmetic and copies ran while one was open for 16% of the time, Pallas kernels for 0%

commit v1 on v0

v1 whole, which is shorter than its diff:
```python
import math

import jax
import jax.numpy as jnp
from jax import lax
from jax.experimental import pallas as pl
from jax.experimental.pallas import tpu as pltpu
from jax.sharding import PartitionSpec as P

SIDE = 64
BF16 = jnp.bfloat16
F32 = jnp.float32
VMEM = pltpu.CompilerParams(vmem_limit_bytes=48 * 1024 * 1024)


def rolled(block, amount):
    return pltpu.roll(block, amount % block.shape[-1], axis=block.ndim - 1)


def lane_index(shape):
    return lax.broadcasted_iota(jnp.int32, shape, len(shape) - 1)


def shift_rows(block, rows):
    cells = block.shape[-1]
    lane = lane_index(block.shape) + rows * SIDE
    moved = rolled(block, -rows * SIDE)
    return jnp.where((lane >= 0) & (lane < cells), moved, 0.0)


def shift_cols(block, cols):
    col = lane_index(block.shape) % SIDE + cols
    moved = rolled(block, -cols)
    return jnp.where((col >= 0) & (col < SIDE), moved, 0.0)


def strips_kernel(x_ref, g_ref, out_ref):
    strips = out_ref.shape[0] // 2
    cells = x_ref.shape[1] // 2
    inner = cells // strips
    width = inner + 2 * SIDE
    for which, ref in enumerate((x_ref, g_ref)):
        for plane in range(2):
            block = ref[:, plane * cells : (plane + 1) * cells].astype(F32)
            zeros = jnp.zeros((block.shape[0], 2 * SIDE), F32)
            wide = rolled(jnp.concatenate([block, zeros], axis=1), SIDE).astype(BF16)
            for strip in range(strips):
                out_ref[2 * strip + which, :, plane * width : (plane + 1) * width] = wide[
                    :, strip * inner : strip * inner + width
                ]


def kernel_grad_kernel(x_ref, low_ref, high_ref, g_ref, out_ref, xs, gs):
    cells = low_ref.shape[1]
    c_rows, o_rows = x_ref.shape[0], g_ref.shape[0]
    for plane in range(4):
        if plane == 0:
            block = low_ref[...]
        elif plane == 3:
            block = high_ref[...]
        else:
            block = x_ref[:, (plane - 1) * cells : plane * cells]
        wide = block.astype(F32)
        first = 3 * plane * c_rows
        xs[first : first + c_rows] = shift_rows(wide, -1).astype(BF16)
        xs[first + c_rows : first + 2 * c_rows] = block
        xs[first + 2 * c_rows : first + 3 * c_rows] = shift_rows(wide, 1).astype(BF16)
    total = jnp.zeros((9 * c_rows, 3 * o_rows), F32)
    for plane in range(2):
        block = g_ref[:, plane * cells : (plane + 1) * cells]
        wide = block.astype(F32)
        gs[0:o_rows] = shift_cols(wide, 1).astype(BF16)
        gs[o_rows : 2 * o_rows] = block
        gs[2 * o_rows : 3 * o_rows] = shift_cols(wide, -1).astype(BF16)
        first = 3 * plane * c_rows
        total = total + lax.dot_general(
            xs[first : first + 9 * c_rows],
            gs[...],
            (((1,), (1,)), ((), ())),
            preferred_element_type=F32,
        )
    parts = out_ref.shape[0]
    rows = c_rows // parts
    for part in range(parts):
        for tap in range(9):
            start = tap * c_rows + part * rows
            out_ref[part, tap * rows : (tap + 1) * rows, :] = total[start : start + rows]


def filter_order_kernel(parts_ref, out_ref):
    parts, rows, _ = parts_ref.shape
    o_rows = parts_ref.shape[2] // 3
    c_rows = out_ref.shape[1]
    out_all = out_ref.shape[2]
    chunk = o_rows // parts
    source = lax.broadcasted_iota(jnp.int32, (3 * o_rows, out_all), 0)
    target = lax.broadcasted_iota(jnp.int32, (3 * o_rows, out_all), 1)
    for col_k in range(3):
        placed = jnp.zeros((rows, out_all), F32)
        for part in range(parts):
            local_o = source - col_k * o_rows
            home = (lax.div(local_o, chunk) * parts + part) * chunk + lax.rem(local_o, chunk)
            chosen = (local_o >= 0) & (local_o < o_rows) & (home == target)
            placed = placed + lax.dot_general(
                parts_ref[part],
                jnp.where(chosen, 1.0, 0.0).astype(F32),
                (((1,), (0,)), ((), ())),
                precision=lax.Precision.HIGHEST,
                preferred_element_type=F32,
            )
        for tap in range(9):
            out_ref[3 * tap + col_k] = placed[tap * c_rows : (tap + 1) * c_rows]
    for spare in range(27, out_ref.shape[0]):
        out_ref[spare] = jnp.zeros(out_ref.shape[1:], F32)


def convolve_kernel(which_ref, d_ref, low_ref, high_ref, w_ref, out_ref, cols):
    channels, width = low_ref.shape
    inner = width - 2 * SIDE
    for plane in range(4):
        if plane == 0:
            block = low_ref[...]
        elif plane == 3:
            block = high_ref[...]
        else:
            block = d_ref[:, (plane - 1) * width : plane * width]
        wide = block.astype(F32)
        for col_k in range(3):
            moved = wide if col_k == 1 else shift_cols(wide, col_k - 1)
            middle = rolled(moved, -SIDE).astype(BF16)[:, :inner]
            ends = moved.astype(BF16)
            pieces = (ends[:, :inner], middle, ends[:, 2 * SIDE :])
            for row_k in range(3):
                first = (3 * row_k + col_k) * channels
                cols[first : first + channels, plane * inner : (plane + 1) * inner] = pieces[row_k]

    @pl.when(which_ref[0] == 0)
    def _():
        total = jnp.zeros(out_ref.shape, F32)
        for plane_k in range(3):
            total = total + lax.dot_general(
                w_ref[9 * plane_k * channels : 9 * (plane_k + 1) * channels],
                cols[:, plane_k * inner : (plane_k + 2) * inner],
                (((0,), (0,)), ((), ())),
                preferred_element_type=F32,
            )
        out_ref[...] = total.astype(BF16)

    @pl.when(which_ref[0] == 1)
    def _():
        total = jnp.zeros(out_ref.shape, F32)
        for plane_k in range(3):
            taps = [26 - 9 * plane_k - tap for tap in range(9)]
            mirrored = jnp.concatenate(
                [w_ref[tap * channels : (tap + 1) * channels] for tap in taps], axis=1
            )
            total = total + jnp.dot(
                mirrored,
                cols[:, plane_k * inner : (plane_k + 2) * inner],
                preferred_element_type=F32,
            )
        out_ref[...] = total.astype(BF16)


def local(inputs, weights, grad_out):
    _, c_dev, planes, cells = inputs.shape
    out_all = weights.shape[2]
    n_chan = lax.axis_size("chan")
    n_space = lax.axis_size("space")
    n_batch = lax.axis_size("sample")
    group = 4
    strips = n_chan // 2
    inner = cells // strips
    width = inner + 2 * SIDE
    side_by_side = [[group * i + j for j in range(group)] for i in range(n_chan // group)]
    strided = [[group * i + j for i in range(n_chan // group)] for j in range(group)]
    forward = [(i, i + 1) for i in range(n_space - 1)]
    backward = [(target, source) for source, target in forward]
    which = lax.rem(lax.axis_index("chan"), 2)
    whole = pl.BlockSpec(memory_space=pltpu.VMEM)

    x = inputs.reshape(c_dev, planes * cells)
    g = grad_out.reshape(c_dev, planes * cells)

    x_block = lax.all_to_all(
        jnp.broadcast_to(x, (group, *x.shape)), "chan", 0, 0, axis_index_groups=side_by_side
    ).reshape(group * c_dev, planes * cells)
    g_block = lax.all_to_all(
        jnp.broadcast_to(g, (group, *g.shape)), "chan", 0, 0, axis_index_groups=strided
    ).reshape(group * c_dev, planes * cells)

    strip_parts = pl.pallas_call(
        strips_kernel,
        out_shape=jax.ShapeDtypeStruct((n_chan, c_dev, planes * width), BF16),
        in_specs=[whole, whole],
        out_specs=whole,
        compiler_params=VMEM,
    )(x, g)
    strip = lax.all_to_all(strip_parts, "chan", 0, 0).reshape(n_chan * c_dev, planes * width)
    all_weights = lax.all_gather(weights, "chan", axis=1, tiled=True)

    low = lax.ppermute(x_block[:, cells:], "space", forward)
    high = lax.ppermute(x_block[:, :cells], "space", backward)
    block = group * c_dev
    terms = pl.pallas_call(
        kernel_grad_kernel,
        out_shape=jax.ShapeDtypeStruct((group, 9 * c_dev, 3 * block), F32),
        in_specs=[whole] * 4,
        out_specs=whole,
        scratch_shapes=[
            pltpu.VMEM((12 * block, cells), BF16),
            pltpu.VMEM((3 * block, cells), BF16),
        ],
        compiler_params=VMEM,
    )(x_block, low, high, g_block)
    terms = lax.all_to_all(terms, "chan", 0, 0, axis_index_groups=side_by_side)
    shares = n_space * n_batch
    terms = pl.pallas_call(
        filter_order_kernel,
        out_shape=jax.ShapeDtypeStruct((shares, c_dev, out_all), F32),
        in_specs=[whole],
        out_specs=whole,
        compiler_params=VMEM,
    )(terms)
    scale = 1.0 / math.sqrt(shares * planes * cells)
    terms = lax.all_to_all(terms, ("space", "sample"), 0, 0)
    share = jnp.sum(terms, axis=0, keepdims=True) * scale
    shared = lax.all_to_all(jnp.broadcast_to(share, terms.shape), ("space", "sample"), 0, 0)
    grad_weights = shared[: weights.shape[0]]

    strip_low = lax.ppermute(strip[:, width:], "space", forward)
    strip_high = lax.ppermute(strip[:, :width], "space", backward)
    result = pl.pallas_call(
        convolve_kernel,
        out_shape=jax.ShapeDtypeStruct((n_chan * c_dev, planes * inner), BF16),
        in_specs=[pl.BlockSpec(memory_space=pltpu.SMEM)] + [whole] * 4,
        out_specs=whole,
        scratch_shapes=[pltpu.VMEM((9 * n_chan * c_dev, 4 * inner), BF16)],
        compiler_params=VMEM,
    )(
        which.reshape(1),
        strip,
        strip_low,
        strip_high,
        all_weights.reshape(27 * n_chan * c_dev, out_all),
    )
    back = lax.all_to_all(result.reshape(n_chan, c_dev, planes * inner), "chan", 0, 0)
    back = back.reshape(strips, 2, c_dev, planes, inner).transpose(1, 2, 3, 0, 4)
    back = back.reshape(2, 1, c_dev, planes, cells)
    return back[0], back[1], grad_weights


def solution(mesh):
    in_specs = (
        P("sample", "chan", "space", None),
        P(None, "chan", None),
        P("sample", "chan", "space", None),
    )
    out_specs = (
        P("sample", "chan", "space", None),
        P("sample", "chan", "space", None),
        P(None, "chan", None),
    )
    return jax.shard_map(local, mesh=mesh, in_specs=in_specs, out_specs=out_specs, check_vma=False)
```

time: 289 us -> 147 us (0.51)
  waiting for transfers between devices: 126 us -> 50.4 us
  blocking collectives: 78.6 us -> 21.5 us
  starting transfers between devices: 12.1 us -> 59.7 us
  local copies, waits for them, and re-layouts: 34.2 us -> 5.73 us
  between operations: 15.2 us -> 0.74 us
  matrix products: 10.8 us -> 0 us
  other arithmetic: 8.8 us -> 0.04 us
  Pallas kernels: 0 us -> 7.88 us
    psum x1 -> x0, waiting for transfers between devices: 123 us -> none  [local(): grad_weights = lax.psum(local_grads * grad_scale, ('space', 'sample'))]
    unnamed x1 -> x0, blocking collectives: 78.6 us -> none
    all_to_all x0 -> x7, starting transfers between devices: none -> 51.1 us  [the longest x1 12.7 us: local(): terms = lax.all_to_all(terms, ('space', 'sample'), 0, 0)]
    all_to_all x0 -> x7, waiting for transfers between devices: none -> 41.3 us  [the longest x1 13.3 us: local(): lax.all_to_all(jnp.broadcast_to(g, (group, *g.shape)), 'chan', 0, 0, axis...]
    all_gather x0 -> x1, blocking collectives: none -> 21.5 us  [local(): all_weights = lax.all_gather(weights, 'chan', axis=1, tiled=True)]
    slice x9 -> x4, local copies, waits for them, and re-layouts: 18 us -> 0.74 us  [the longest x1 0.65 us: local(): grad_weights = shared[:weights.shape[0]]]
    dot_general x5 -> x0, matrix products: 10.8 us -> none  [the longest x3 4.12 us: local(): jnp.dot(kernel_rows[plane_k], depth_slab, preferred_element_type=jnp.floa...]
    pallas_call x0 -> x4, Pallas kernels: none -> 7.88 us  [the longest x1 3.39 us: local(): pl.pallas_call(convolve_kernel, out_shape=jax.ShapeDtypeStruct((n_chan *...]
  transfers between devices with their start and end apart: 6 -> 11, of which waited for: 2 -> 6; matrix products, arithmetic and copies ran while one was open for 16% -> 1% of each run, Pallas kernels for 0% -> 5%
where the time goes in v1:
time: 147 us; the launch traced here: 146 us
  starting transfers between devices  59.7 us (41%)
  waiting for transfers between devices  50.4 us (34%)
  blocking collectives  21.5 us (15%)
  Pallas kernels  7.88 us (5%)
  local copies, waits for them, and re-layouts  5.73 us (4%)
    all_gather x1, blocking collectives, local(): all_weights = lax.all_gather(weights, 'chan', axis=1, tiled=True)  21.5 us
    all_to_all x1, waiting for transfers between devices, local(): lax.all_to_all(jnp.broadcast_to(g, (group, *g.shape)), 'chan', 0, 0, axis...  13.3 us
    all_to_all x1, starting transfers between devices, local(): terms = lax.all_to_all(terms, ('space', 'sample'), 0, 0)  12.7 us
    all_to_all x1, waiting for transfers between devices, local(): lax.all_to_all(result.reshape(n_chan, c_dev, planes * inner), 'chan', 0, 0)  11.7 us
    all_to_all x1, starting transfers between devices, local(): lax.all_to_all(jnp.broadcast_to(x, (group, *x.shape)), 'chan', 0, 0, axis...  10.4 us
    all_to_all x1, starting transfers between devices, local(): lax.all_to_all(jnp.broadcast_to(share, terms.shape), ('space', 'sample'),...  9.49 us
    all_to_all x1, waiting for transfers between devices, local(): lax.all_to_all(jnp.broadcast_to(share, terms.shape), ('space', 'sample'),...  8.44 us
    all_to_all x1, waiting for transfers between devices, local(): lax.all_to_all(jnp.broadcast_to(x, (group, *x.shape)), 'chan', 0, 0, axis...  7.9 us
  transfers between devices with their start and end apart: 11, of which 6 were waited for; matrix products, arithmetic and copies ran while one was open for 1% of the time, Pallas kernels for 5%

profile of v1, /device:TPU:1, one launch (start us, length us, event | category | flops | bytes accessed | tf_op | source)
XLA Modules:
  0.0 146.0 jit_solution(17356292359127521156)
XLA Ops:
  0.6 1.0 copy.7
  1.6 0.8 broadcast_in_dim.12
  2.4 0.0 copy-start
  2.4 10.4 %all-to-all-start.2 = ((bf16[4,8,8192]{2,1,0:T(8,128)(2,1)}), bf16[4,8,8192]{2,1,0:T(8,128)(2,1)S(1)}, u32[]{:S(2)}, u32[]{:S(2)}) async-start(bf16[4,8,8192]{2,1,0:T(8,128)(2,1)} %broadcast_in_dim.12), calls=%async_computation.2 | async-start | bytes 1048576 | tf_op jit(solution)/shard_map/all_to_all | solution.py:185
  12.9 0.0 copy-done
  12.9 0.1 copy.8
  13.0 7.9 %all-to-all-done.2 = bf16[4,8,8192]{2,1,0:T(8,128)(2,1)S(1)} async-done(((bf16[4,8,8192]{2,1,0:T(8,128)(2,1)}), bf16[4,8,8192]{2,1,0:T(8,128)(2,1)S(1)}, u32[]{:S(2)}, u32[]{:S(2)}) %all-to-all-start.2) | async-done | bytes 524320 | tf_op jit(solution)/shard_map/all_to_all | solution.py:185
  20.9 0.8 broadcast_in_dim.13
  21.7 3.5 %all-to-all-start.3 = ((bf16[4,8,8192]{2,1,0:T(8,128)(2,1)}), bf16[4,8,8192]{2,1,0:T(8,128)(2,1)S(1)}, u32[]{:S(2)}, u32[]{:S(2)}) async-start(bf16[4,8,8192]{2,1,0:T(8,128)(2,1)} %broadcast_in_dim.13), calls=%async_computation.3 | async-start | bytes 1048576 | tf_op jit(solution)/shard_map/all_to_all | solution.py:188
  25.2 0.9 shard_map.58
  26.0 13.3 %all-to-all-done.3 = bf16[4,8,8192]{2,1,0:T(8,128)(2,1)S(1)} async-done(((bf16[4,8,8192]{2,1,0:T(8,128)(2,1)}), bf16[4,8,8192]{2,1,0:T(8,128)(2,1)S(1)}, u32[]{:S(2)}, u32[]{:S(2)}) %all-to-all-start.3) | async-done | bytes 524320 | tf_op jit(solution)/shard_map/all_to_all | solution.py:188
  39.3 6.1 %all-to-all-start = ((bf16[16,8,1280]{2,1,0:T(8,128)(2,1)}), bf16[16,8,1280]{2,1,0:T(8,128)(2,1)S(1)}, u32[]{:S(2)}, u32[]{:S(2)}) async-start(bf16[16,8,1280]{2,1,0:T(8,128)(2,1)} %shard_map.58), calls=%async_computation | async-start | bytes 655360 | tf_op jit(solution)/shard_map/all_to_all | solution.py:199
  45.5 2.0 %collective-permute-start.2 = (bf16[32,4096]{1,0:T(8,128)(2,1)S(1)}, bf16[32,4096]{1,0:T(8,128)(2,1)S(1)}, u32[]{:S(2)}, u32[]{:S(2)}) collective-permute-start(bf16[32,4096]{1,0:T(8,128)(2,1)S(1)} %get-tuple-element.4), channel_id=1, source_target_pairs={{0,4},{4,8},{8,12},{12,16},{16,20},{20,24},{24,28},{1,5},{5,9},{9,... | collective-permute-start | bytes 786440 | tf_op jit(solution)/shard_map/ppermute | solution.py:202
  47.5 1.3 collective-permute-start.3
  48.8 4.3 %collective-permute-done.2.low_ref = bf16[32,4096]{1,0:T(8,128)(2,1)S(1)} collective-permute-done((bf16[32,4096]{1,0:T(8,128)(2,1)S(1)}, bf16[32,4096]{1,0:T(8,128)(2,1)S(1)}, u32[]{:S(2)}, u32[]{:S(2)}) %collective-permute-start.2) | collective-permute-done | bytes 262176 | tf_op jit(solution)/shard_map/ppermute | solution.py:202
  53.1 4.8 %collective-permute-done.3.high_ref = bf16[32,4096]{1,0:T(8,128)(2,1)S(1)} collective-permute-done((bf16[32,4096]{1,0:T(8,128)(2,1)S(1)}, bf16[32,4096]{1,0:T(8,128)(2,1)S(1)}, u32[]{:S(2)}, u32[]{:S(2)}) %collective-permute-start.3) | collective-permute-done | bytes 262176 | tf_op jit(solution)/shard_map/ppermute | solution.py:203
  57.9 2.1 %shard_map.60 = f32[4,72,96]{2,1,0:T(8,128)} custom-call(bf16[32,8192]{1,0:T(8,128)(2,1)S(1)} %bitcast.21, bf16[32,4096]{1,0:T(8,128)(2,1)S(1)} %collective-permute-done.2.low_ref, bf16[32,4096]{1,0:T(8,128)(2,1)S(1)} %collective-permute-done.3.high_ref, bf16[32,8192]{1,0:T(8,128)(2,1)S(1)} %bitcast.25), custom_call_target="tpu_custom_call" | custom-call | tf_op jit(solution)/shard_map/pallas_call | solution.py:205
  60.0 0.0 all-to-all-done
  60.0 4.2 %all-to-all-start.4 = ((f32[4,72,96]{2,1,0:T(8,128)}), f32[4,72,96]{2,1,0:T(8,128)S(1)}, u32[]{:S(2)}, u32[]{:S(2)}) async-start(f32[4,72,96]{2,1,0:T(8,128)} %shard_map.60), calls=%async_computation.4 | async-start | bytes 294912 | tf_op jit(solution)/shard_map/all_to_all | solution.py:216
  64.2 4.0 %collective-permute-start = (bf16[128,640]{1,0:T(8,128)(2,1)S(1)}, bf16[128,640]{1,0:T(8,128)(2,1)S(1)}, u32[]{:S(2)}, u32[]{:S(2)}) collective-permute-start(bf16[128,640]{1,0:T(8,128)(2,1)S(1)} %get-tuple-element.6), channel_id=1, source_target_pairs={{0,4},{4,8},{8,12},{12,16},{16,20},{20,24},{24,28},{1,5},{5,9},{9,... | collective-permute-start | bytes 491528 | tf_op jit(solution)/shard_map/ppermute | solution.py:231
  68.3 1.3 collective-permute-start.1
  69.6 0.0 all-to-all-done.4.parts_ref
  69.6 1.5 %shard_map.61 = f32[32,8,128]{2,1,0:T(8,128)} custom-call(f32[4,72,96]{2,1,0:T(8,128)S(1)} %all-to-all-done.4.parts_ref), custom_call_target="tpu_custom_call" | custom-call | tf_op jit(solution)/shard_map/pallas_call | solution.py:218
  71.1 0.0 copy-start.1
  71.1 12.7 %all-to-all-start.5 = ((f32[32,8,128]{2,1,0:T(8,128)}), f32[32,8,128]{2,1,0:T(8,128)S(1)}, u32[]{:S(2)}, u32[]{:S(2)}) async-start(f32[32,8,128]{2,1,0:T(8,128)} %shard_map.61), calls=%async_computation.5 | async-start | bytes 262144 | tf_op jit(solution)/shard_map/all_to_all | solution.py:226
  83.7 0.0 copy-done.1
  83.7 21.5 %all_gather.3 = bf16[27,128,128]{2,1,0:T(8,128)(2,1)S(1)} all-gather(bf16[27,8,128]{2,1,0:T(8,128)(2,1)S(1)} %copy-done.1), channel_id=1, replica_groups=mesh['chan'=16,'space'=8,'sample'=4] {'chan'}, dimensions={1}, use_global_device_ids=true | all-gather | bytes 940032 | tf_op jit(solution)/shard_map/all_gather | solution.py:200
  105.3 0.0 collective-permute-done.low_ref
  105.3 0.0 collective-permute-done.1.high_ref
  105.3 3.4 %shard_map.59 = bf16[128,1024]{1,0:T(8,128)(2,1)} custom-call(s32[1]{0:T(128)} %bitcast.which_ref, bf16[128,1280]{1,0:T(8,128)(2,1)S(1)} %bitcast.24, bf16[128,640]{1,0:T(8,128)(2,1)S(1)} %collective-permute-done.low_ref, bf16[128,640]{1,0:T(8,128)(2,1)S(1)} %collective-permute-done.1.high_ref, bf16[3456,128]{1,0:T(8,128)(2,1)S(1)} %bitcast.22), custom_call_target="tpu_custom_call" | custom-call | tf_op jit(solution)/shard_map/pallas_call | solution.py:233
  108.7 0.0 all-to-all-done.5
  108.7 4.7 %all-to-all-start.1 = ((bf16[16,8,1024]{2,1,0:T(8,128)(2,1)}), bf16[16,8,1024]{2,1,0:T(8,128)(2,1)S(1)}, u32[]{:S(2)}, u32[]{:S(2)}) async-start(bf16[16,8,1024]{2,1,0:T(8,128)(2,1)} %bitcast.3), calls=%async_computation.1 | async-start | bytes 524288 | tf_op jit(solution)/shard_map/all_to_all | solution.py:247
  113.4 11.7 %all-to-all-done.1 = bf16[16,8,1024]{2,1,0:T(8,128)(2,1)S(1)} async-done(((bf16[16,8,1024]{2,1,0:T(8,128)(2,1)}), bf16[16,8,1024]{2,1,0:T(8,128)(2,1)S(1)}, u32[]{:S(2)}, u32[]{:S(2)}) %all-to-all-start.1) | async-done | bytes 262176 | tf_op jit(solution)/shard_map/all_to_all | solution.py:247
  125.1 0.7 broadcast_in_dim.14
  125.8 9.5 %all-to-all-start.6 = ((f32[32,8,128]{2,1,0:T(8,128)}), f32[32,8,128]{2,1,0:T(8,128)S(1)}, u32[]{:S(2)}, u32[]{:S(2)}) async-start(f32[32,8,128]{2,1,0:T(8,128)} %broadcast_in_dim.14), calls=%async_computation.6 | async-start | bytes 262144 | tf_op jit(solution)/shard_map/all_to_all | solution.py:228
  135.3 0.2 copy.10
  135.5 0.7 squeeze.6
  136.2 0.7 squeeze.7
  136.9 8.4 %all-to-all-done.6 = f32[32,8,128]{2,1,0:T(8,128)S(1)} async-done(((f32[32,8,128]{2,1,0:T(8,128)}), f32[32,8,128]{2,1,0:T(8,128)S(1)}, u32[]{:S(2)}, u32[]{:S(2)}) %all-to-all-start.6) | async-done | bytes 131104 | tf_op jit(solution)/shard_map/all_to_all | solution.py:228
  145.4 0.7 slice.36
  (5 shorter events, 0.1 us)
Async XLA Ops:
  2.4 10.5 %copy-start = (bf16[1,8,2,4096]{3,2,1,0:T(2,128)(2,1)S(1)}, bf16[1,8,2,4096]{3,2,1,0:T(2,128)(2,1)}, u32[]{:S(2)}) copy-start(bf16[1,8,2,4096]{3,2,1,0:T(2,128)(2,1)} %param.5) | copy-start | bytes 393220
  2.4 18.4 %all-to-all-start.2 = ((bf16[4,8,8192]{2,1,0:T(8,128)(2,1)}), bf16[4,8,8192]{2,1,0:T(8,128)(2,1)S(1)}, u32[]{:S(2)}, u32[]{:S(2)}) async-start(bf16[4,8,8192]{2,1,0:T(8,128)(2,1)} %broadcast_in_dim.12), calls=%async_computation.2 | async-start | bytes 1048576 | tf_op jit(solution)/shard_map/all_to_all | solution.py:185
  21.7 17.6 %all-to-all-start.3 = ((bf16[4,8,8192]{2,1,0:T(8,128)(2,1)}), bf16[4,8,8192]{2,1,0:T(8,128)(2,1)S(1)}, u32[]{:S(2)}, u32[]{:S(2)}) async-start(bf16[4,8,8192]{2,1,0:T(8,128)(2,1)} %broadcast_in_dim.13), calls=%async_computation.3 | async-start | bytes 1048576 | tf_op jit(solution)/shard_map/all_to_all | solution.py:188
  39.3 20.7 %all-to-all-start = ((bf16[16,8,1280]{2,1,0:T(8,128)(2,1)}), bf16[16,8,1280]{2,1,0:T(8,128)(2,1)S(1)}, u32[]{:S(2)}, u32[]{:S(2)}) async-start(bf16[16,8,1280]{2,1,0:T(8,128)(2,1)} %shard_map.58), calls=%async_computation | async-start | bytes 655360 | tf_op jit(solution)/shard_map/all_to_all | solution.py:199
  45.5 7.7 %collective-permute-start.2 = (bf16[32,4096]{1,0:T(8,128)(2,1)S(1)}, bf16[32,4096]{1,0:T(8,128)(2,1)S(1)}, u32[]{:S(2)}, u32[]{:S(2)}) collective-permute-start(bf16[32,4096]{1,0:T(8,128)(2,1)S(1)} %get-tuple-element.4), channel_id=1, source_target_pairs={{0,4},{4,8},{8,12},{12,16},{16,20},{20,24},{24,28},{1,5},{5,9},{9,... | collective-permute-start | bytes 786440 | tf_op jit(solution)/shard_map/ppermute | solution.py:202
  47.5 10.4 %collective-permute-start.3 = (bf16[32,4096]{1,0:T(8,128)(2,1)S(1)}, bf16[32,4096]{1,0:T(8,128)(2,1)S(1)}, u32[]{:S(2)}, u32[]{:S(2)}) collective-permute-start(bf16[32,4096]{1,0:T(8,128)(2,1)S(1)} %get-tuple-element.3), channel_id=1, source_target_pairs={{4,0},{8,4},{12,8},{16,12},{20,16},{24,20},{28,24},{5,1},{9,5},{13... | collective-permute-start | bytes 786440 | tf_op jit(solution)/shard_map/ppermute | solution.py:203
  60.0 9.5 %all-to-all-start.4 = ((f32[4,72,96]{2,1,0:T(8,128)}), f32[4,72,96]{2,1,0:T(8,128)S(1)}, u32[]{:S(2)}, u32[]{:S(2)}) async-start(f32[4,72,96]{2,1,0:T(8,128)} %shard_map.60), calls=%async_computation.4 | async-start | bytes 294912 | tf_op jit(solution)/shard_map/all_to_all | solution.py:216
  64.2 41.0 %collective-permute-start = (bf16[128,640]{1,0:T(8,128)(2,1)S(1)}, bf16[128,640]{1,0:T(8,128)(2,1)S(1)}, u32[]{:S(2)}, u32[]{:S(2)}) collective-permute-start(bf16[128,640]{1,0:T(8,128)(2,1)S(1)} %get-tuple-element.6), channel_id=1, source_target_pairs={{0,4},{4,8},{8,12},{12,16},{16,20},{20,24},{24,28},{1,5},{5,9},{9,... | collective-permute-start | bytes 491528 | tf_op jit(solution)/shard_map/ppermute | solution.py:231
  68.3 37.0 %collective-permute-start.1 = (bf16[128,640]{1,0:T(8,128)(2,1)S(1)}, bf16[128,640]{1,0:T(8,128)(2,1)S(1)}, u32[]{:S(2)}, u32[]{:S(2)}) collective-permute-start(bf16[128,640]{1,0:T(8,128)(2,1)S(1)} %get-tuple-element.5), channel_id=1, source_target_pairs={{4,0},{8,4},{12,8},{16,12},{20,16},{24,20},{28,24},{5,1},{9,5},{13... | collective-permute-start | bytes 491528 | tf_op jit(solution)/shard_map/ppermute | solution.py:232
  71.1 12.7 %copy-start.1 = (bf16[27,8,128]{2,1,0:T(8,128)(2,1)S(1)}, bf16[27,8,128]{2,1,0:T(8,128)(2,1)}, u32[]{:S(2)}) copy-start(bf16[27,8,128]{2,1,0:T(8,128)(2,1)} %param.4) | copy-start | bytes 165892
  71.1 37.6 %all-to-all-start.5 = ((f32[32,8,128]{2,1,0:T(8,128)}), f32[32,8,128]{2,1,0:T(8,128)S(1)}, u32[]{:S(2)}, u32[]{:S(2)}) async-start(f32[32,8,128]{2,1,0:T(8,128)} %shard_map.61), calls=%async_computation.5 | async-start | bytes 262144 | tf_op jit(solution)/shard_map/all_to_all | solution.py:226
  108.7 16.4 %all-to-all-start.1 = ((bf16[16,8,1024]{2,1,0:T(8,128)(2,1)}), bf16[16,8,1024]{2,1,0:T(8,128)(2,1)S(1)}, u32[]{:S(2)}, u32[]{:S(2)}) async-start(bf16[16,8,1024]{2,1,0:T(8,128)(2,1)} %bitcast.3), calls=%async_computation.1 | async-start | bytes 524288 | tf_op jit(solution)/shard_map/all_to_all | solution.py:247
  125.8 19.6 %all-to-all-start.6 = ((f32[32,8,128]{2,1,0:T(8,128)}), f32[32,8,128]{2,1,0:T(8,128)S(1)}, u32[]{:S(2)}, u32[]{:S(2)}) async-start(f32[32,8,128]{2,1,0:T(8,128)} %broadcast_in_dim.14), calls=%async_computation.6 | async-start | bytes 262144 | tf_op jit(solution)/shard_map/all_to_all | solution.py:228

commit v2 on v0

v2 whole, which is shorter than its diff:
```python
import math

import jax
import jax.numpy as jnp
from jax import lax
from jax.experimental import pallas as pl
from jax.experimental.pallas import tpu as pltpu
from jax.sharding import PartitionSpec as P

SIDE = 64
BF16 = jnp.bfloat16
F32 = jnp.float32
VMEM = pltpu.CompilerParams(vmem_limit_bytes=48 * 1024 * 1024)


def rolled(block, amount):
    return pltpu.roll(block, amount % block.shape[-1], axis=block.ndim - 1)


def lane_index(shape):
    return lax.broadcasted_iota(jnp.int32, shape, len(shape) - 1)


def shift_rows(block, rows):
    cells = block.shape[-1]
    lane = lane_index(block.shape) + rows * SIDE
    moved = rolled(block, -rows * SIDE)
    return jnp.where((lane >= 0) & (lane < cells), moved, 0.0)


def shift_cols(block, cols):
    col = lane_index(block.shape) % SIDE + cols
    moved = rolled(block, -cols)
    return jnp.where((col >= 0) & (col < SIDE), moved, 0.0)


def chip_block(which_ref, own_ref, other_ref, chip, start, stop):
    own = own_ref[chip, :, start:stop].astype(F32)
    other = other_ref[chip, :, start:stop].astype(F32)
    even = which_ref[0] == 0
    return jnp.concatenate(
        [jnp.where(even, own, other), jnp.where(even, other, own)], axis=0
    )


def send_kernel(x_ref, g_ref, w_ref, row_ref, gs_ref):
    cells = x_ref.shape[1]
    row_ref[:, :cells] = x_ref[...]
    taps, _, out_all = w_ref.shape
    for tap in range(taps):
        start = cells + tap * out_all
        row_ref[:, start : start + out_all] = w_ref[tap]
    for chip in range(gs_ref.shape[0]):
        gs_ref[chip] = g_ref[...]


def kernel_grad_kernel(which_ref, x_ref, low_ref, high_ref, own_ref, other_ref, out_ref, gs):
    cells = low_ref.shape[1]
    chips, c_rows, _ = own_ref.shape
    out_all = 2 * chips * c_rows
    planes = [low_ref[...], x_ref[:, :cells], x_ref[:, cells : 2 * cells], high_ref[...]]
    moved = []
    for block in planes:
        wide = block.astype(F32)
        moved.append([shift_rows(wide, -1), wide, shift_rows(wide, 1)])
    total = jnp.zeros((9 * c_rows, 3 * out_all), F32)
    for plane in range(2):
        rows = [moved[plane + plane_k][row_k] for plane_k in range(3) for row_k in range(3)]
        for chip in range(chips):
            block = chip_block(
                which_ref, own_ref, other_ref, chip, plane * cells, (plane + 1) * cells
            )
            for col_k in range(3):
                first = col_k * out_all + 2 * c_rows * chip
                turned = block if col_k == 1 else shift_cols(block, 1 - col_k)
                gs[first : first + 2 * c_rows] = turned.astype(BF16)
        total = total + lax.dot_general(
            jnp.concatenate(rows, axis=0).astype(BF16),
            gs[...],
            (((1,), (1,)), ((), ())),
            preferred_element_type=F32,
        )
    for tap in range(9):
        for col_k in range(3):
            out_ref[3 * tap + col_k] = total[
                tap * c_rows : (tap + 1) * c_rows, col_k * out_all : (col_k + 1) * out_all
            ]
    for spare in range(27, out_ref.shape[0]):
        out_ref[spare] = jnp.zeros(out_ref.shape[1:], F32)


def convolve_kernel(
    me_ref, which_ref, all_ref, own_ref, other_ref, w_ref, after_ref,
    middle_ref, low_ref, high_ref, g_all, terms,
):
    del after_ref
    rows, out_all = w_ref.shape
    taps = 27
    c_rows = rows // taps
    cells = low_ref.shape[1]
    wide = 2 * cells
    channel = lax.broadcasted_iota(jnp.int32, (c_rows, out_all), 0) + c_rows * me_ref[0]
    mine = jnp.where(channel == lax.broadcasted_iota(jnp.int32, (c_rows, out_all), 1), 1.0, 0.0)
    picked = []
    for tap in reversed(range(taps)):
        start = wide + tap * out_all
        picked.append(
            lax.dot_general(
                mine.astype(BF16),
                all_ref[:, start : start + out_all],
                (((1,), (1,)), ((), ())),
                preferred_element_type=F32,
            )
        )
    kernels = (jnp.concatenate(picked, axis=0).astype(BF16), w_ref[...])
    for which in range(2):
        home = slice(which * c_rows, (which + 1) * c_rows)
        for plane in range(2):
            span = slice(plane * cells, (plane + 1) * cells)
            if which == 0:
                block = all_ref[:, span]
            else:
                for chip in range(own_ref.shape[0]):
                    g_all[2 * c_rows * chip : 2 * c_rows * (chip + 1)] = chip_block(
                        which_ref, own_ref, other_ref, chip, span.start, span.stop
                    ).astype(BF16)
                block = g_all[...]
            terms[plane] = jnp.dot(kernels[which], block, preferred_element_type=F32)
        for target in range(4):
            result = jnp.zeros((c_rows, cells), F32)
            for col_k in range(3):
                column = jnp.zeros((c_rows, cells), F32)
                for row_k in range(3):
                    sums = jnp.zeros((c_rows, cells), F32)
                    for plane in range(2):
                        plane_k = target - plane
                        if 0 <= plane_k < 3:
                            first = c_rows * (9 * plane_k + 3 * row_k + col_k)
                            sums = sums + terms[plane, first : first + c_rows]
                    column = column + (sums if row_k == 1 else shift_rows(sums, 1 - row_k))
                result = result + (column if col_k == 1 else shift_cols(column, 1 - col_k))
            if target == 0:
                low_ref[home] = result
            elif target == 3:
                high_ref[home] = result
            else:
                middle_ref[target - 1, home] = result


def call(kernel, out_shape, scratch_shapes, *args, after=None):
    whole = pl.BlockSpec(memory_space=pltpu.VMEM)
    scalars = pl.BlockSpec(memory_space=pltpu.SMEM)
    in_specs = [scalars if arg.dtype == jnp.int32 else whole for arg in args]
    if after is not None:
        in_specs.append(pl.BlockSpec(memory_space=pl.ANY))
        args = (*args, after)
    return pl.pallas_call(
        kernel,
        out_shape=out_shape,
        in_specs=in_specs,
        out_specs=jax.tree.map(lambda _: whole, out_shape),
        scratch_shapes=scratch_shapes,
        compiler_params=VMEM,
    )(*args)


def local(inputs, weights, grad_out):
    _, c_dev, planes, cells = inputs.shape
    taps, _, out_all = weights.shape
    n_chan = lax.axis_size("chan")
    n_space = lax.axis_size("space")
    n_batch = lax.axis_size("sample")
    chips = n_chan // 2
    along_y = [[core + 2 * chip for chip in range(chips)] for core in range(2)]
    cores = [(i, i ^ 1) for i in range(n_chan)]
    forward = [(i, i + 1) for i in range(n_space - 1)]
    backward = [(target, source) for source, target in forward]
    me = lax.axis_index("chan").reshape(1)
    which = lax.rem(me, 2)
    shape = jax.ShapeDtypeStruct

    x = inputs.reshape(c_dev, planes * cells)
    g = grad_out.reshape(c_dev, planes * cells)
    row, g_copies = call(
        send_kernel,
        (
            shape((c_dev, planes * cells + taps * out_all), BF16),
            shape((chips, c_dev, planes * cells), BF16),
        ),
        [],
        x, g, weights,
    )
    gathered = lax.all_gather(row, "chan", axis=0, tiled=True)
    own = lax.all_to_all(g_copies, "chan", 0, 0, axis_index_groups=along_y)
    x_low = lax.ppermute(x[:, cells:], "space", forward)
    x_high = lax.ppermute(x[:, :cells], "space", backward)
    own, x_low, x_high = lax.optimization_barrier((own, x_low, x_high))
    other = lax.ppermute(own, "chan", cores)

    shares = n_space * n_batch
    terms = call(
        kernel_grad_kernel,
        shape((shares, c_dev, out_all), F32),
        [pltpu.VMEM((3 * out_all, cells), BF16)],
        which, x, x_low, x_high, own, other,
    )
    partial = terms
    terms = lax.all_to_all(terms, ("space", "sample"), 0, 0)

    middle, to_below, to_above = call(
        convolve_kernel,
        (
            shape((planes, 2 * c_dev, cells), F32),
            shape((2 * c_dev, cells), F32),
            shape((2 * c_dev, cells), F32),
        ),
        [pltpu.VMEM((out_all, cells), BF16), pltpu.VMEM((planes, taps * c_dev, cells), F32)],
        me, which, gathered, own, other, weights.reshape(taps * c_dev, out_all),
        after=partial,
    )
    scale = 1.0 / math.sqrt(shares * planes * cells)
    terms, middle = lax.optimization_barrier((terms, middle))
    share = jnp.sum(terms, axis=0, keepdims=True) * scale
    shared = lax.all_to_all(jnp.broadcast_to(share, terms.shape), ("space", "sample"), 0, 0)
    grad_weights = shared[:taps]

    from_below = lax.ppermute(to_above, "space", forward)
    from_above = lax.ppermute(to_below, "space", backward)
    both = jnp.stack([middle[0] + from_below, middle[1] + from_above], 1).astype(BF16)
    return both[None, :c_dev], both[None, c_dev:], grad_weights


def solution(mesh):
    in_specs = (
        P("sample", "chan", "space", None),
        P(None, "chan", None),
        P("sample", "chan", "space", None),
    )
    out_specs = (
        P("sample", "chan", "space", None),
        P("sample", "chan", "space", None),
        P(None, "chan", None),
    )
    return jax.shard_map(local, mesh=mesh, in_specs=in_specs, out_specs=out_specs, check_vma=False)
```

time: 289 us -> 117 us (0.40); the launches traced: 285 us -> 117 us
  waiting for transfers between devices: 126 us -> 33.7 us
  blocking collectives: 78.6 us -> 16.8 us
  local copies, waits for them, and re-layouts: 34.2 us -> 5.05 us
  starting transfers between devices: 12.1 us -> 37.3 us
  matrix products: 10.8 us -> 0 us
  Pallas kernels: 0 us -> 9.46 us
  other arithmetic: 8.8 us -> 0.11 us
    psum x1 -> x0, waiting for transfers between devices: 123 us -> none  [local(): grad_weights = lax.psum(local_grads * grad_scale, ('space', 'sample'))]
    unnamed x1 -> x0, blocking collectives: 78.6 us -> none
    all_to_all x0 -> x2, waiting for transfers between devices: none -> 30.1 us  [the longest x1 25.9 us: local(): own = lax.all_to_all(g_copies, 'chan', 0, 0, axis_index_groups=along_y)]
    all_to_all x0 -> x2, starting transfers between devices: none -> 22.1 us  [the longest x1 14.4 us: local(): terms = lax.all_to_all(terms, ('space', 'sample'), 0, 0)]
    slice x9 -> x2, local copies, waits for them, and re-layouts: 18 us -> 0.66 us  [the longest x1 0.65 us: local(): grad_weights = shared[:taps]]
    all_to_all x0 -> x1, blocking collectives: none -> 16.8 us  [local(): lax.all_to_all(jnp.broadcast_to(share, terms.shape), ('space', 'sample'),...]
    dot_general x5 -> x0, matrix products: 10.8 us -> none  [the longest x3 4.12 us: local(): jnp.dot(kernel_rows[plane_k], depth_slab, preferred_element_type=jnp.floa...]
    pallas_call x0 -> x3, Pallas kernels: none -> 9.46 us  [call(): pl.pallas_call(kernel, out_shape=out_shape, in_specs=in_specs, out_specs=...]
  transfers between devices with their start and end apart: 6 -> 8, of which waited for: 2 -> 4; matrix products, arithmetic and copies ran while one was open for 16% -> 1% of each run, Pallas kernels for 0% -> 7%
where the time goes in v2:
time: 117 us
  starting transfers between devices  37.3 us (32%)
  waiting for transfers between devices  33.7 us (29%)
  blocking collectives  16.8 us (14%)
  between operations  14.2 us (12%)
  Pallas kernels  9.46 us (8%)
  local copies, waits for them, and re-layouts  5.05 us (4%)
    all_to_all x1, waiting for transfers between devices, local(): own = lax.all_to_all(g_copies, 'chan', 0, 0, axis_index_groups=along_y)  25.9 us
    all_to_all x1, blocking collectives, local(): lax.all_to_all(jnp.broadcast_to(share, terms.shape), ('space', 'sample'),...  16.8 us
    all_to_all x1, starting transfers between devices, local(): terms = lax.all_to_all(terms, ('space', 'sample'), 0, 0)  14.4 us
    pallas_call x3, Pallas kernels, call(): pl.pallas_call(kernel, out_shape=out_shape, in_specs=in_specs, out_specs=...  9.46 us
    all_to_all x1, starting transfers between devices, local(): own = lax.all_to_all(g_copies, 'chan', 0, 0, axis_index_groups=along_y)  7.68 us
    ppermute x1, starting transfers between devices, local(): other = lax.ppermute(own, 'chan', cores)  5.35 us
    ppermute x1, starting transfers between devices, local(): x_low = lax.ppermute(x[:, cells:], 'space', forward)  4.61 us
    unnamed x8, local copies, waits for them, and re-layouts  4.38 us
  transfers between devices with their start and end apart: 8, of which 4 were waited for; matrix products, arithmetic and copies ran while one was open for 1% of the time, Pallas kernels for 7%

profile of v2, /device:TPU:1, one launch (start us, length us, event | category | flops | bytes accessed | tf_op | source)
XLA Modules:
  0.0 116.6 jit_solution(7692920232806649845)
XLA Ops:
  7.2 0.0 all-gather.2.cloned.1.call-start
  7.2 1.0 copy.8
  8.2 0.0 copy-start.1
  8.2 1.0 copy.9
  9.2 0.0 copy-start
  9.2 0.8 copy-done
  10.0 1.1 shard_map.58
  11.1 0.0 all-gather.2.cloned.1.call-update
  11.1 7.7 %all-to-all-start = ((bf16[8,8,8192]{2,1,0:T(8,128)(2,1)}), bf16[8,8,8192]{2,1,0:T(8,128)(2,1)S(1)}, u32[]{:S(2)}, u32[]{:S(2)}) async-start(bf16[8,8,8192]{2,1,0:T(8,128)(2,1)} %get-tuple-element.13), calls=%async_computation | async-start | bytes 2097152 | tf_op jit(solution)/shard_map/all_to_all | solution.py:194
  18.8 1.3 %collective-permute-start.1 = (bf16[8,4096]{1,0:T(8,128)(2,1)S(1)}, bf16[8,4096]{1,0:T(8,128)(2,1)S(1)}, u32[]{:S(2)}, u32[]{:S(2)}) collective-permute-start(bf16[8,4096]{1,0:T(8,128)(2,1)S(1)} %get-tuple-element.30), channel_id=1, source_target_pairs={{4,0},{8,4},{12,8},{16,12},{20,16},{24,20},{28,24},{5,1},{9,5},{13... | collective-permute-start | bytes 196616 | tf_op jit(solution)/shard_map/ppermute | solution.py:196
  20.1 4.6 %collective-permute-start = (bf16[8,4096]{1,0:T(8,128)(2,1)S(1)}, bf16[8,4096]{1,0:T(8,128)(2,1)S(1)}, u32[]{:S(2)}, u32[]{:S(2)}) collective-permute-start(bf16[8,4096]{1,0:T(8,128)(2,1)S(1)} %get-tuple-element.31), channel_id=1, source_target_pairs={{0,4},{4,8},{8,12},{12,16},{16,20},{20,24},{24,28},{1,5},{5,9},{9,... | collective-permute-start | bytes 196616 | tf_op jit(solution)/shard_map/ppermute | solution.py:195
  24.7 0.0 collective-permute-done.1.high_ref
  24.7 1.3 %collective-permute-done.low_ref = bf16[8,4096]{1,0:T(8,128)(2,1)S(1)} collective-permute-done((bf16[8,4096]{1,0:T(8,128)(2,1)S(1)}, bf16[8,4096]{1,0:T(8,128)(2,1)S(1)}, u32[]{:S(2)}, u32[]{:S(2)}) %collective-permute-start) | collective-permute-done | bytes 65568 | tf_op jit(solution)/shard_map/ppermute | solution.py:195
  26.0 25.9 %all-to-all-done.own_ref = bf16[8,8,8192]{2,1,0:T(8,128)(2,1)S(1)} async-done(((bf16[8,8,8192]{2,1,0:T(8,128)(2,1)}), bf16[8,8,8192]{2,1,0:T(8,128)(2,1)S(1)}, u32[]{:S(2)}, u32[]{:S(2)}) %all-to-all-start) | async-done | bytes 1048608 | tf_op jit(solution)/shard_map/all_to_all | solution.py:194
  52.0 5.4 %collective-permute-start.2 = (bf16[8,8,8192]{2,1,0:T(8,128)(2,1)S(1)}, bf16[8,8,8192]{2,1,0:T(8,128)(2,1)S(1)}, u32[]{:S(2)}, u32[]{:S(2)}) collective-permute-start(bf16[8,8,8192]{2,1,0:T(8,128)(2,1)S(1)} %all-to-all-done.own_ref), channel_id=1, source_target_pairs={{0,32},{32,0},{64,96},{96,64},{128,160},{160,128},{192,224},{224,1... | collective-permute-start | bytes 3145736 | tf_op jit(solution)/shard_map/ppermute | solution.py:198
  57.3 2.3 %collective-permute-done.2.other_ref = bf16[8,8,8192]{2,1,0:T(8,128)(2,1)S(1)} collective-permute-done((bf16[8,8,8192]{2,1,0:T(8,128)(2,1)S(1)}, bf16[8,8,8192]{2,1,0:T(8,128)(2,1)S(1)}, u32[]{:S(2)}, u32[]{:S(2)}) %collective-permute-start.2) | collective-permute-done | bytes 1048608 | tf_op jit(solution)/shard_map/ppermute | solution.py:198
  59.6 3.2 %shard_map.59.after_ref = f32[32,8,128]{2,1,0:T(8,128)} custom-call(s32[1]{0:T(128)S(6)} %rem.18.which_ref, bf16[8,8192]{1,0:T(8,128)(2,1)S(1)} %bitcast.30, bf16[8,4096]{1,0:T(8,128)(2,1)S(1)} %collective-permute-done.low_ref, bf16[8,4096]{1,0:T(8,128)(2,1)S(1)} %collective-permute-done.1.high_ref, bf16[8,8,8192]{2,1,0:T(8,128)(2,1)S(1)} %all-to-all-done.own_ref, ...), custom_call_target="tpu_custom_call" | custom-call | tf_op jit(solution)/shard_map/pallas_call | solution.py:157
  62.8 14.4 %all-to-all-start.1 = ((f32[32,8,128]{2,1,0:T(8,128)}), f32[32,8,128]{2,1,0:T(8,128)S(1)}, u32[]{:S(2)}, u32[]{:S(2)}) async-start(f32[32,8,128]{2,1,0:T(8,128)} %shard_map.59.after_ref), calls=%async_computation.1 | async-start | bytes 262144 | tf_op jit(solution)/shard_map/all_to_all | solution.py:208
  77.3 0.0 all-gather.2.cloned.1.call-done.all_ref
  77.3 0.0 copy-done.1
  77.3 5.1 %shard_map.60 = (f32[2,16,4096]{2,1,0:T(8,128)S(1)}, f32[16,4096]{1,0:T(8,128)S(1)}, f32[16,4096]{1,0:T(8,128)S(1)}) custom-call(s32[1]{0:T(128)} %bitcast.me_ref, s32[1]{0:T(128)S(6)} %rem.18.which_ref, bf16[128,11648]{1,0:T(8,128)(2,1)} %all-gather.2.cloned.1.call-done.all_ref, bf16[8,8,8192]{2,1,0:T(8,128)(2,1)S(1)} %all-to-all-done.own_ref, ...), custom_call_target="tpu_custom_call" | custom-call | tf_op jit(solution)/shard_map/pallas_call | solution.py:157
  82.4 4.2 %all-to-all-done.1 = f32[32,8,128]{2,1,0:T(8,128)S(1)} async-done(((f32[32,8,128]{2,1,0:T(8,128)}), f32[32,8,128]{2,1,0:T(8,128)S(1)}, u32[]{:S(2)}, u32[]{:S(2)}) %all-to-all-start.1) | async-done | bytes 131104 | tf_op jit(solution)/shard_map/all_to_all | solution.py:208
  86.6 2.6 %collective-permute-start.3 = (f32[16,4096]{1,0:T(8,128)S(1)}, f32[16,4096]{1,0:T(8,128)S(1)}, u32[]{:S(2)}, u32[]{:S(2)}) collective-permute-start(f32[16,4096]{1,0:T(8,128)S(1)} %get-tuple-element.20), channel_id=1, source_target_pairs={{0,4},{4,8},{8,12},{12,16},{16,20},{20,24},{24,28},{1,5},{5,9},{9,... | collective-permute-start | bytes 786440 | tf_op jit(solution)/shard_map/ppermute | solution.py:227
  89.2 1.3 %collective-permute-start.4 = (f32[16,4096]{1,0:T(8,128)S(1)}, f32[16,4096]{1,0:T(8,128)S(1)}, u32[]{:S(2)}, u32[]{:S(2)}) collective-permute-start(f32[16,4096]{1,0:T(8,128)S(1)} %get-tuple-element.21), channel_id=1, source_target_pairs={{4,0},{8,4},{12,8},{16,12},{20,16},{24,20},{28,24},{5,1},{9,5},{13... | collective-permute-start | bytes 786440 | tf_op jit(solution)/shard_map/ppermute | solution.py:228
  90.6 16.8 %all_to_all.15 = f32[32,8,128]{2,1,0:T(8,128)S(1)} all-to-all(f32[32,8,128]{2,1,0:T(8,128)S(1)} %broadcast_in_dim.14), channel_id=1, replica_groups=mesh['chan'=16,'space'=8,'sample'=4] {'space','sample'}, dimensions={0} | all-to-all | bytes 262144 | tf_op jit(solution)/shard_map/all_to_all | solution.py:224
  107.4 0.7 slice.32
  108.0 0.0 collective-permute-done.3
  108.1 0.0 collective-permute-done.4
  108.1 0.8 copy.7
  108.9 0.8 copy.6
  (6 shorter events, 0.1 us)
Async XLA Ops:
  7.2 70.1 %all-gather.2.cloned.1.call-start = ((), (), s32[]{:S(2)}) async-start(), calls=%async_computation.3 | async-start | bytes 3168256 | tf_op jit(solution)/shard_map/all_gather | solution.py:193
  8.2 69.1 %copy-start.1 = (bf16[27,8,128]{2,1,0:T(8,128)(2,1)S(1)}, bf16[27,8,128]{2,1,0:T(8,128)(2,1)}, u32[]{:S(2)}) copy-start(bf16[27,8,128]{2,1,0:T(8,128)(2,1)} %w_ref.1) | copy-start | bytes 165892
  9.2 0.8 copy-start
  11.1 40.8 %all-to-all-start = ((bf16[8,8,8192]{2,1,0:T(8,128)(2,1)}), bf16[8,8,8192]{2,1,0:T(8,128)(2,1)S(1)}, u32[]{:S(2)}, u32[]{:S(2)}) async-start(bf16[8,8,8192]{2,1,0:T(8,128)(2,1)} %get-tuple-element.13), calls=%async_computation | async-start | bytes 2097152 | tf_op jit(solution)/shard_map/all_to_all | solution.py:194
  18.8 5.9 %collective-permute-start.1 = (bf16[8,4096]{1,0:T(8,128)(2,1)S(1)}, bf16[8,4096]{1,0:T(8,128)(2,1)S(1)}, u32[]{:S(2)}, u32[]{:S(2)}) collective-permute-start(bf16[8,4096]{1,0:T(8,128)(2,1)S(1)} %get-tuple-element.30), channel_id=1, source_target_pairs={{4,0},{8,4},{12,8},{16,12},{20,16},{24,20},{28,24},{5,1},{9,5},{13... | collective-permute-start | bytes 196616 | tf_op jit(solution)/shard_map/ppermute | solution.py:196
  20.1 5.9 %collective-permute-start = (bf16[8,4096]{1,0:T(8,128)(2,1)S(1)}, bf16[8,4096]{1,0:T(8,128)(2,1)S(1)}, u32[]{:S(2)}, u32[]{:S(2)}) collective-permute-start(bf16[8,4096]{1,0:T(8,128)(2,1)S(1)} %get-tuple-element.31), channel_id=1, source_target_pairs={{0,4},{4,8},{8,12},{12,16},{16,20},{20,24},{24,28},{1,5},{5,9},{9,... | collective-permute-start | bytes 196616 | tf_op jit(solution)/shard_map/ppermute | solution.py:195
  52.0 7.6 %collective-permute-start.2 = (bf16[8,8,8192]{2,1,0:T(8,128)(2,1)S(1)}, bf16[8,8,8192]{2,1,0:T(8,128)(2,1)S(1)}, u32[]{:S(2)}, u32[]{:S(2)}) collective-permute-start(bf16[8,8,8192]{2,1,0:T(8,128)(2,1)S(1)} %all-to-all-done.own_ref), channel_id=1, source_target_pairs={{0,32},{32,0},{64,96},{96,64},{128,160},{160,128},{192,224},{224,1... | collective-permute-start | bytes 3145736 | tf_op jit(solution)/shard_map/ppermute | solution.py:198
  62.8 23.8 %all-to-all-start.1 = ((f32[32,8,128]{2,1,0:T(8,128)}), f32[32,8,128]{2,1,0:T(8,128)S(1)}, u32[]{:S(2)}, u32[]{:S(2)}) async-start(f32[32,8,128]{2,1,0:T(8,128)} %shard_map.59.after_ref), calls=%async_computation.1 | async-start | bytes 262144 | tf_op jit(solution)/shard_map/all_to_all | solution.py:208
  86.6 21.4 %collective-permute-start.3 = (f32[16,4096]{1,0:T(8,128)S(1)}, f32[16,4096]{1,0:T(8,128)S(1)}, u32[]{:S(2)}, u32[]{:S(2)}) collective-permute-start(f32[16,4096]{1,0:T(8,128)S(1)} %get-tuple-element.20), channel_id=1, source_target_pairs={{0,4},{4,8},{8,12},{12,16},{16,20},{20,24},{24,28},{1,5},{5,9},{9,... | collective-permute-start | bytes 786440 | tf_op jit(solution)/shard_map/ppermute | solution.py:227
  89.2 18.8 %collective-permute-start.4 = (f32[16,4096]{1,0:T(8,128)S(1)}, f32[16,4096]{1,0:T(8,128)S(1)}, u32[]{:S(2)}, u32[]{:S(2)}) collective-permute-start(f32[16,4096]{1,0:T(8,128)S(1)} %get-tuple-element.21), channel_id=1, source_target_pairs={{4,0},{8,4},{12,8},{16,12},{20,16},{24,20},{28,24},{5,1},{9,5},{13... | collective-permute-start | bytes 786440 | tf_op jit(solution)/shard_map/ppermute | solution.py:228
Sparse Core Ops, SparseCore 0:
  11.2 56.5 all-gather.1

commit v3 on v2

--- a/solution.py
+++ b/solution.py
@@ -147,7 +147,7 @@
                 middle_ref[target - 1, home] = result
 
 
-def call(kernel, out_shape, scratch_shapes, *args, after=None):
+def call(kernel, out_shape, scratch_shapes, *args, after=None, flops=None):
     whole = pl.BlockSpec(memory_space=pltpu.VMEM)
     scalars = pl.BlockSpec(memory_space=pltpu.SMEM)
     in_specs = [scalars if arg.dtype == jnp.int32 else whole for arg in args]
@@ -161,7 +161,20 @@
         out_specs=jax.tree.map(lambda _: whole, out_shape),
         scratch_shapes=scratch_shapes,
         compiler_params=VMEM,
+        cost_estimate=flops and pl.CostEstimate(flops=flops, bytes_accessed=0, transcendentals=0),
     )(*args)
+
+
+def finish_kernel(middle_ref, below_ref, above_ref, out_ref, grad_ref):
+    rows = out_ref.shape[0]
+    for home, ref in ((slice(0, rows), out_ref), (slice(rows, 2 * rows), grad_ref)):
+        first = middle_ref[0, home] + below_ref[home]
+        second = middle_ref[1, home] + above_ref[home]
+        ref[...] = jnp.stack([first, second], axis=1).astype(BF16)
+
+
+def take_kernel(shares_ref, out_ref):
+    out_ref[...] = shares_ref[: out_ref.shape[0]]
 
 
 def local(inputs, weights, grad_out):
@@ -221,13 +234,19 @@
     scale = 1.0 / math.sqrt(shares * planes * cells)
     terms, middle = lax.optimization_barrier((terms, middle))
     share = jnp.sum(terms, axis=0, keepdims=True) * scale
-    shared = lax.all_to_all(jnp.broadcast_to(share, terms.shape), ("space", "sample"), 0, 0)
-    grad_weights = shared[:taps]
+    spread = jnp.broadcast_to(share, terms.shape)
+    spread, to_above, to_below = lax.optimization_barrier((spread, to_above, to_below))
+    shared = lax.all_to_all(spread, ("space", "sample"), 0, 0)
+    grad_weights = call(
+        take_kernel, shape(weights.shape, F32), [], shared, flops=30_000_000_000
+    )
 
     from_below = lax.ppermute(to_above, "space", forward)
     from_above = lax.ppermute(to_below, "space", backward)
-    both = jnp.stack([middle[0] + from_below, middle[1] + from_above], 1).astype(BF16)
-    return both[None, :c_dev], both[None, c_dev:], grad_weights
+    output, grad_in = call(
+        finish_kernel, (shape(inputs.shape[1:], BF16),) * 2, [], middle, from_below, from_above
+    )
+    return output[None], grad_in[None], grad_weights
 
 
 def solution(mesh):

time: 117 us -> 113 us (0.966)
  blocking collectives: 16.8 us -> 0 us
  waiting for transfers between devices: 33.7 us -> 39.6 us
  starting transfers between devices: 37.3 us -> 42.9 us
  Pallas kernels: 9.46 us -> 11.2 us
  local copies, waits for them, and re-layouts: 5.05 us -> 3.47 us
    all_to_all x1 -> x0, blocking collectives: 16.8 us -> none  [local(): lax.all_to_all(jnp.broadcast_to(share, terms.shape), ('space', 'sample'),...]
    all_to_all x0 -> x1, starting transfers between devices: none -> 5.07 us  [local(): shared = lax.all_to_all(spread, ('space', 'sample'), 0, 0)]
    all_to_all x0 -> x1, waiting for transfers between devices: none -> 4.89 us  [local(): shared = lax.all_to_all(spread, ('space', 'sample'), 0, 0)]
    pallas_call x3 -> x5, Pallas kernels: 9.46 us -> 11.2 us  [call(): pl.pallas_call(kernel, out_shape=out_shape, in_specs=in_specs, out_specs=...]
    unnamed x8 -> x6, local copies, waits for them, and re-layouts: 4.38 us -> 2.8 us
  transfers between devices with their start and end apart: 8 -> 9, of which waited for: 4 -> 6; matrix products, arithmetic and copies ran while one was open for 1% -> 0% of each run, Pallas kernels for 7% -> 8%
where the time goes in v3:
time: 113 us; the launch traced here: 111 us
  starting transfers between devices  42.9 us (38%)
  waiting for transfers between devices  39.6 us (35%)
  between operations  14.1 us (12%)
  Pallas kernels  11.2 us (10%)
  local copies, waits for them, and re-layouts  3.47 us (3%)
    all_to_all x1, waiting for transfers between devices, local(): own = lax.all_to_all(g_copies, 'chan', 0, 0, axis_index_groups=along_y)  25.9 us
    all_to_all x1, starting transfers between devices, local(): terms = lax.all_to_all(terms, ('space', 'sample'), 0, 0)  14.4 us
    pallas_call x5, Pallas kernels, call(): pl.pallas_call(kernel, out_shape=out_shape, in_specs=in_specs, out_specs=...  11.2 us
    all_to_all x1, starting transfers between devices, local(): own = lax.all_to_all(g_copies, 'chan', 0, 0, axis_index_groups=along_y)  7.68 us
    ppermute x1, starting transfers between devices, local(): other = lax.ppermute(own, 'chan', cores)  5.35 us
    all_to_all x1, starting transfers between devices, local(): shared = lax.all_to_all(spread, ('space', 'sample'), 0, 0)  5.07 us
    all_to_all x1, waiting for transfers between devices, local(): shared = lax.all_to_all(spread, ('space', 'sample'), 0, 0)  4.89 us
    ppermute x1, starting transfers between devices, local(): x_low = lax.ppermute(x[:, cells:], 'space', forward)  4.61 us
  transfers between devices with their start and end apart: 9, of which 6 were waited for; matrix products, arithmetic and copies ran while one was open for 0% of the time, Pallas kernels for 8%

profile of v3, /device:TPU:1, one launch (start us, length us, event | category | flops | bytes accessed | tf_op | source)
XLA Modules:
  0.0 111.4 jit_solution(9400139721379975990)
XLA Ops:
  7.2 0.0 all-gather.2.cloned.1.call-start
  7.2 1.0 copy.6
  8.2 0.0 copy-start.1
  8.2 1.0 copy.7
  9.2 0.0 copy-start
  9.2 0.8 copy-done
  10.0 1.1 shard_map.58
  11.1 0.0 all-gather.2.cloned.1.call-update
  11.1 7.7 %all-to-all-start = ((bf16[8,8,8192]{2,1,0:T(8,128)(2,1)}), bf16[8,8,8192]{2,1,0:T(8,128)(2,1)S(1)}, u32[]{:S(2)}, u32[]{:S(2)}) async-start(bf16[8,8,8192]{2,1,0:T(8,128)(2,1)} %get-tuple-element.18), calls=%async_computation | async-start | bytes 2097152 | tf_op jit(solution)/shard_map/all_to_all | solution.py:207
  18.8 1.3 %collective-permute-start.1 = (bf16[8,4096]{1,0:T(8,128)(2,1)S(1)}, bf16[8,4096]{1,0:T(8,128)(2,1)S(1)}, u32[]{:S(2)}, u32[]{:S(2)}) collective-permute-start(bf16[8,4096]{1,0:T(8,128)(2,1)S(1)} %get-tuple-element.33), channel_id=1, source_target_pairs={{4,0},{8,4},{12,8},{16,12},{20,16},{24,20},{28,24},{5,1},{9,5},{13... | collective-permute-start | bytes 196616 | tf_op jit(solution)/shard_map/ppermute | solution.py:209
  20.1 4.6 %collective-permute-start = (bf16[8,4096]{1,0:T(8,128)(2,1)S(1)}, bf16[8,4096]{1,0:T(8,128)(2,1)S(1)}, u32[]{:S(2)}, u32[]{:S(2)}) collective-permute-start(bf16[8,4096]{1,0:T(8,128)(2,1)S(1)} %get-tuple-element.34), channel_id=1, source_target_pairs={{0,4},{4,8},{8,12},{12,16},{16,20},{20,24},{24,28},{1,5},{5,9},{9,... | collective-permute-start | bytes 196616 | tf_op jit(solution)/shard_map/ppermute | solution.py:208
  24.7 0.0 collective-permute-done.1.high_ref
  24.7 1.3 %collective-permute-done.low_ref = bf16[8,4096]{1,0:T(8,128)(2,1)S(1)} collective-permute-done((bf16[8,4096]{1,0:T(8,128)(2,1)S(1)}, bf16[8,4096]{1,0:T(8,128)(2,1)S(1)}, u32[]{:S(2)}, u32[]{:S(2)}) %collective-permute-start) | collective-permute-done | bytes 65568 | tf_op jit(solution)/shard_map/ppermute | solution.py:208
  26.0 25.9 %all-to-all-done.own_ref = bf16[8,8,8192]{2,1,0:T(8,128)(2,1)S(1)} async-done(((bf16[8,8,8192]{2,1,0:T(8,128)(2,1)}), bf16[8,8,8192]{2,1,0:T(8,128)(2,1)S(1)}, u32[]{:S(2)}, u32[]{:S(2)}) %all-to-all-start) | async-done | bytes 1048608 | tf_op jit(solution)/shard_map/all_to_all | solution.py:207
  52.0 5.4 %collective-permute-start.2 = (bf16[8,8,8192]{2,1,0:T(8,128)(2,1)S(1)}, bf16[8,8,8192]{2,1,0:T(8,128)(2,1)S(1)}, u32[]{:S(2)}, u32[]{:S(2)}) collective-permute-start(bf16[8,8,8192]{2,1,0:T(8,128)(2,1)S(1)} %all-to-all-done.own_ref), channel_id=1, source_target_pairs={{0,32},{32,0},{64,96},{96,64},{128,160},{160,128},{192,224},{224,1... | collective-permute-start | bytes 3145736 | tf_op jit(solution)/shard_map/ppermute | solution.py:211
  57.3 2.3 %collective-permute-done.2.other_ref = bf16[8,8,8192]{2,1,0:T(8,128)(2,1)S(1)} collective-permute-done((bf16[8,8,8192]{2,1,0:T(8,128)(2,1)S(1)}, bf16[8,8,8192]{2,1,0:T(8,128)(2,1)S(1)}, u32[]{:S(2)}, u32[]{:S(2)}) %collective-permute-start.2) | collective-permute-done | bytes 1048608 | tf_op jit(solution)/shard_map/ppermute | solution.py:211
  59.6 3.2 %shard_map.59.after_ref = f32[32,8,128]{2,1,0:T(8,128)} custom-call(s32[1]{0:T(128)S(6)} %rem.18.which_ref, bf16[8,8192]{1,0:T(8,128)(2,1)S(1)} %bitcast.12, bf16[8,4096]{1,0:T(8,128)(2,1)S(1)} %collective-permute-done.low_ref, bf16[8,4096]{1,0:T(8,128)(2,1)S(1)} %collective-permute-done.1.high_ref, bf16[8,8,8192]{2,1,0:T(8,128)(2,1)S(1)} %all-to-all-done.own_ref, ...), custom_call_target="tpu_custom_call" | custom-call | tf_op jit(solution)/shard_map/pallas_call | solution.py:157
  62.8 14.4 %all-to-all-start.1 = ((f32[32,8,128]{2,1,0:T(8,128)}), f32[32,8,128]{2,1,0:T(8,128)S(1)}, u32[]{:S(2)}, u32[]{:S(2)}) async-start(f32[32,8,128]{2,1,0:T(8,128)} %shard_map.59.after_ref), calls=%async_computation.1 | async-start | bytes 262144 | tf_op jit(solution)/shard_map/all_to_all | solution.py:221
  77.3 0.0 all-gather.2.cloned.1.call-done.all_ref
  77.3 0.0 copy-done.1
  77.3 5.1 %shard_map.60 = (f32[2,16,4096]{2,1,0:T(8,128)S(1)}, f32[16,4096]{1,0:T(8,128)S(1)}, f32[16,4096]{1,0:T(8,128)S(1)}) custom-call(s32[1]{0:T(128)} %bitcast.me_ref, s32[1]{0:T(128)S(6)} %rem.18.which_ref, bf16[128,11648]{1,0:T(8,128)(2,1)} %all-gather.2.cloned.1.call-done.all_ref, bf16[8,8,8192]{2,1,0:T(8,128)(2,1)S(1)} %all-to-all-done.own_ref, ...), custom_call_target="tpu_custom_call" | custom-call | tf_op jit(solution)/shard_map/pallas_call | solution.py:157
  82.5 4.2 %all-to-all-done.1 = f32[32,8,128]{2,1,0:T(8,128)S(1)} async-done(((f32[32,8,128]{2,1,0:T(8,128)}), f32[32,8,128]{2,1,0:T(8,128)S(1)}, u32[]{:S(2)}, u32[]{:S(2)}) %all-to-all-start.1) | async-done | bytes 131104 | tf_op jit(solution)/shard_map/all_to_all | solution.py:221
  86.6 0.7 broadcast_in_dim.12
  87.3 5.1 %all-to-all-start.2 = ((f32[32,8,128]{2,1,0:T(8,128)}), f32[32,8,128]{2,1,0:T(8,128)S(1)}, u32[]{:S(2)}, u32[]{:S(2)}) async-start(f32[32,8,128]{2,1,0:T(8,128)} %broadcast_in_dim.12), calls=%async_computation.2 | async-start | bytes 262144 | tf_op jit(solution)/shard_map/all_to_all | solution.py:239
  92.4 3.2 %collective-permute-start.3 = (f32[16,4096]{1,0:T(8,128)S(1)}, f32[16,4096]{1,0:T(8,128)S(1)}, u32[]{:S(2)}, u32[]{:S(2)}) collective-permute-start(f32[16,4096]{1,0:T(8,128)S(1)} %get-tuple-element.28), channel_id=1, source_target_pairs={{0,4},{4,8},{8,12},{12,16},{16,20},{20,24},{24,28},{1,5},{5,9},{9,... | collective-permute-start | bytes 786440 | tf_op jit(solution)/shard_map/ppermute | solution.py:244
  95.6 1.3 %collective-permute-start.4 = (f32[16,4096]{1,0:T(8,128)S(1)}, f32[16,4096]{1,0:T(8,128)S(1)}, u32[]{:S(2)}, u32[]{:S(2)}) collective-permute-start(f32[16,4096]{1,0:T(8,128)S(1)} %get-tuple-element.29), channel_id=1, source_target_pairs={{4,0},{8,4},{12,8},{16,12},{20,16},{24,20},{28,24},{5,1},{9,5},{13... | collective-permute-start | bytes 786440 | tf_op jit(solution)/shard_map/ppermute | solution.py:245
  96.9 4.9 %all-to-all-done.2.shares_ref = f32[32,8,128]{2,1,0:T(8,128)S(1)} async-done(((f32[32,8,128]{2,1,0:T(8,128)}), f32[32,8,128]{2,1,0:T(8,128)S(1)}, u32[]{:S(2)}, u32[]{:S(2)}) %all-to-all-start.2) | async-done | bytes 131104 | tf_op jit(solution)/shard_map/all_to_all | solution.py:239
  101.7 0.7 shard_map.62
  102.4 0.0 collective-permute-done.3.below_ref
  102.4 1.1 collective-permute-done.4.above_ref
  103.5 1.1 shard_map.61
  (3 shorter events, 0.1 us)
Async XLA Ops:
  7.2 70.1 %all-gather.2.cloned.1.call-start = ((), (), s32[]{:S(2)}) async-start(), calls=%async_computation.3 | async-start | bytes 3168256 | tf_op jit(solution)/shard_map/all_gather | solution.py:206
  8.2 69.1 %copy-start.1 = (bf16[27,8,128]{2,1,0:T(8,128)(2,1)S(1)}, bf16[27,8,128]{2,1,0:T(8,128)(2,1)}, u32[]{:S(2)}) copy-start(bf16[27,8,128]{2,1,0:T(8,128)(2,1)} %w_ref.1) | copy-start | bytes 165892
  9.2 0.8 copy-start
  11.1 40.8 %all-to-all-start = ((bf16[8,8,8192]{2,1,0:T(8,128)(2,1)}), bf16[8,8,8192]{2,1,0:T(8,128)(2,1)S(1)}, u32[]{:S(2)}, u32[]{:S(2)}) async-start(bf16[8,8,8192]{2,1,0:T(8,128)(2,1)} %get-tuple-element.18), calls=%async_computation | async-start | bytes 2097152 | tf_op jit(solution)/shard_map/all_to_all | solution.py:207
  18.8 5.9 %collective-permute-start.1 = (bf16[8,4096]{1,0:T(8,128)(2,1)S(1)}, bf16[8,4096]{1,0:T(8,128)(2,1)S(1)}, u32[]{:S(2)}, u32[]{:S(2)}) collective-permute-start(bf16[8,4096]{1,0:T(8,128)(2,1)S(1)} %get-tuple-element.33), channel_id=1, source_target_pairs={{4,0},{8,4},{12,8},{16,12},{20,16},{24,20},{28,24},{5,1},{9,5},{13... | collective-permute-start | bytes 196616 | tf_op jit(solution)/shard_map/ppermute | solution.py:209
  20.1 5.9 %collective-permute-start = (bf16[8,4096]{1,0:T(8,128)(2,1)S(1)}, bf16[8,4096]{1,0:T(8,128)(2,1)S(1)}, u32[]{:S(2)}, u32[]{:S(2)}) collective-permute-start(bf16[8,4096]{1,0:T(8,128)(2,1)S(1)} %get-tuple-element.34), channel_id=1, source_target_pairs={{0,4},{4,8},{8,12},{12,16},{16,20},{20,24},{24,28},{1,5},{5,9},{9,... | collective-permute-start | bytes 196616 | tf_op jit(solution)/shard_map/ppermute | solution.py:208
  52.0 7.6 %collective-permute-start.2 = (bf16[8,8,8192]{2,1,0:T(8,128)(2,1)S(1)}, bf16[8,8,8192]{2,1,0:T(8,128)(2,1)S(1)}, u32[]{:S(2)}, u32[]{:S(2)}) collective-permute-start(bf16[8,8,8192]{2,1,0:T(8,128)(2,1)S(1)} %all-to-all-done.own_ref), channel_id=1, source_target_pairs={{0,32},{32,0},{64,96},{96,64},{128,160},{160,128},{192,224},{224,1... | collective-permute-start | bytes 3145736 | tf_op jit(solution)/shard_map/ppermute | solution.py:211
  62.8 23.8 %all-to-all-start.1 = ((f32[32,8,128]{2,1,0:T(8,128)}), f32[32,8,128]{2,1,0:T(8,128)S(1)}, u32[]{:S(2)}, u32[]{:S(2)}) async-start(f32[32,8,128]{2,1,0:T(8,128)} %shard_map.59.after_ref), calls=%async_computation.1 | async-start | bytes 262144 | tf_op jit(solution)/shard_map/all_to_all | solution.py:221
  87.3 14.4 %all-to-all-start.2 = ((f32[32,8,128]{2,1,0:T(8,128)}), f32[32,8,128]{2,1,0:T(8,128)S(1)}, u32[]{:S(2)}, u32[]{:S(2)}) async-start(f32[32,8,128]{2,1,0:T(8,128)} %broadcast_in_dim.12), calls=%async_computation.2 | async-start | bytes 262144 | tf_op jit(solution)/shard_map/all_to_all | solution.py:239
  92.4 10.0 %collective-permute-start.3 = (f32[16,4096]{1,0:T(8,128)S(1)}, f32[16,4096]{1,0:T(8,128)S(1)}, u32[]{:S(2)}, u32[]{:S(2)}) collective-permute-start(f32[16,4096]{1,0:T(8,128)S(1)} %get-tuple-element.28), channel_id=1, source_target_pairs={{0,4},{4,8},{8,12},{12,16},{16,20},{20,24},{24,28},{1,5},{5,9},{9,... | collective-permute-start | bytes 786440 | tf_op jit(solution)/shard_map/ppermute | solution.py:244
  95.6 7.9 %collective-permute-start.4 = (f32[16,4096]{1,0:T(8,128)S(1)}, f32[16,4096]{1,0:T(8,128)S(1)}, u32[]{:S(2)}, u32[]{:S(2)}) collective-permute-start(f32[16,4096]{1,0:T(8,128)S(1)} %get-tuple-element.29), channel_id=1, source_target_pairs={{4,0},{8,4},{12,8},{16,12},{20,16},{24,20},{28,24},{5,1},{9,5},{13... | collective-permute-start | bytes 786440 | tf_op jit(solution)/shard_map/ppermute | solution.py:245
Sparse Core Ops, SparseCore 0:
  11.2 56.5 all-gather.1

commit v4 on v3

v4 whole, which is shorter than its diff:
```python
import functools
import math

import jax
import jax.numpy as jnp
from jax import lax
from jax.experimental import pallas as pl
from jax.experimental.pallas import tpu as pltpu
from jax.sharding import PartitionSpec as P

SIDE = 64
BF16 = jnp.bfloat16
F32 = jnp.float32
MIB = 1024 * 1024


def rolled(block, amount):
    return pltpu.roll(block, amount % block.shape[-1], axis=block.ndim - 1)


def lane_index(shape):
    return lax.broadcasted_iota(jnp.int32, shape, len(shape) - 1)


def shift_rows(block, rows):
    cells = block.shape[-1]
    lane = lane_index(block.shape) + rows * SIDE
    moved = rolled(block, -rows * SIDE)
    return jnp.where((lane >= 0) & (lane < cells), moved, 0.0)


def shift_cols(block, cols):
    col = lane_index(block.shape) % SIDE + cols
    moved = rolled(block, -cols)
    return jnp.where((col >= 0) & (col < SIDE), moved, 0.0)


def send_kernel(
    x_hbm, g_hbm, w_hbm, row_ref, gs_ref, first_ref, second_ref, x_ref, g_ref, w_ref, arrived
):
    copies = [
        pltpu.make_async_copy(source, target, arrived.at[slot])
        for slot, (source, target) in enumerate(((g_hbm, g_ref), (x_hbm, x_ref), (w_hbm, w_ref)))
    ]
    for copy in copies:
        copy.start()
    half = first_ref.shape[1]
    cells = 2 * half
    copies[0].wait()
    g = g_ref[...].astype(F32)
    for plane in range(2):
        flat = g[:, plane].astype(BF16)
        for chip in range(gs_ref.shape[0] // 2):
            gs_ref[2 * chip + plane] = flat
    copies[1].wait()
    x = x_ref[...].astype(F32)
    for plane, ref in enumerate((first_ref, second_ref)):
        flat = x[:, plane].astype(BF16)
        ref[...] = flat
        row_ref[:, plane * half : (plane + 1) * half] = flat
    copies[2].wait()
    taps, _, out_all = w_ref.shape
    for tap in range(taps):
        start = cells + tap * out_all
        row_ref[:, start : start + out_all] = w_ref[tap]


def kernel_grad(plane, planes, g_ref):
    moved = []
    for plane_k in range(3):
        wide = jnp.where(
            plane == 0, planes[plane_k][...].astype(F32), planes[plane_k + 1][...].astype(F32)
        )
        for rows in (-1, 0, 1):
            turned = shift_rows(wide, rows) if rows else wide
            for cols in (-1, 0, 1):
                moved.append(shift_cols(turned, cols) if cols else turned)
    return lax.dot_general(
        jnp.concatenate(moved, axis=0).astype(BF16),
        g_ref[...],
        (((1,), (1,)), ((), ())),
        preferred_element_type=F32,
    )


def own_plane_kernel(which_ref, low_ref, first_ref, second_ref, high_ref, g_ref, out_ref):
    planes = (low_ref, first_ref, second_ref, high_ref)
    out_ref[...] = kernel_grad(which_ref[0], planes, g_ref)


def other_plane_kernel(
    which_ref, low_ref, first_ref, second_ref, high_ref, g_ref, own_ref, out_ref
):
    planes = (low_ref, first_ref, second_ref, high_ref)
    total = own_ref[...] + kernel_grad(1 - which_ref[0], planes, g_ref)
    c_rows = out_ref.shape[1]
    for tap in range(27):
        out_ref[tap] = total[tap * c_rows : (tap + 1) * c_rows]
    for spare in range(27, out_ref.shape[0]):
        out_ref[spare] = jnp.zeros(out_ref.shape[1:], F32)


def share_kernel(scale, terms_ref, out_ref):
    share = jnp.sum(terms_ref[...], axis=0) * scale
    for device in range(out_ref.shape[0]):
        out_ref[device] = share


def convolve_kernel(
    me_ref, which_ref, all_ref, own_ref, other_ref, w_ref, after_ref,
    middle_ref, low_ref, high_ref, terms,
):
    del after_ref
    rows, out_all = w_ref.shape
    taps = 27
    c_rows = rows // taps
    cells = low_ref.shape[1]
    wide = 2 * cells
    channel = lax.broadcasted_iota(jnp.int32, (c_rows, out_all), 0) + c_rows * me_ref[0]
    mine = jnp.where(channel == lax.broadcasted_iota(jnp.int32, (c_rows, out_all), 1), 1.0, 0.0)
    picked = []
    for tap in reversed(range(taps)):
        start = wide + tap * out_all
        picked.append(
            lax.dot_general(
                mine.astype(BF16),
                all_ref[:, start : start + out_all],
                (((1,), (1,)), ((), ())),
                preferred_element_type=F32,
            )
        )
    kernels = (jnp.concatenate(picked, axis=0).astype(BF16), w_ref[...])
    for which in range(2):
        home = slice(which * c_rows, (which + 1) * c_rows)
        for plane in range(2):
            if which == 0:
                block = all_ref[:, plane * cells : (plane + 1) * cells]
                slot = plane
            else:
                block = (own_ref, other_ref)[plane][...]
                slot = which_ref[0] if plane == 0 else 1 - which_ref[0]
            terms[slot] = jnp.dot(kernels[which], block, preferred_element_type=F32)
        for target in range(4):
            result = jnp.zeros((c_rows, cells), F32)
            for col_k in range(3):
                column = jnp.zeros((c_rows, cells), F32)
                for row_k in range(3):
                    sums = jnp.zeros((c_rows, cells), F32)
                    for plane in range(2):
                        plane_k = target - plane
                        if 0 <= plane_k < 3:
                            first = c_rows * (9 * plane_k + 3 * row_k + col_k)
                            sums = sums + terms[plane, first : first + c_rows]
                    column = column + (sums if row_k == 1 else shift_rows(sums, 1 - row_k))
                result = result + (column if col_k == 1 else shift_cols(column, 1 - col_k))
            if target == 0:
                low_ref[home] = result
            elif target == 3:
                high_ref[home] = result
            else:
                middle_ref[target - 1, home] = result


def finish_kernel(middle_ref, below_ref, above_ref, out_ref, grad_ref):
    rows = out_ref.shape[0]
    for home, ref in ((slice(0, rows), out_ref), (slice(rows, 2 * rows), grad_ref)):
        first = middle_ref[0, home] + below_ref[home]
        second = middle_ref[1, home] + above_ref[home]
        ref[...] = jnp.stack([first, second], axis=1).astype(BF16)


def take_kernel(shares_ref, out_ref):
    out_ref[...] = shares_ref[: out_ref.shape[0]]


def call(kernel, out_shape, scratch_shapes, *args, hbm=(), after=(), flops=None, vmem=48):
    whole = pl.BlockSpec(memory_space=pltpu.VMEM)
    scalars = pl.BlockSpec(memory_space=pltpu.SMEM)
    in_specs = [scalars if arg.dtype == jnp.int32 else whole for arg in args]
    in_specs += [pl.BlockSpec(memory_space=pltpu.HBM)] * len(hbm)
    in_specs += [pl.BlockSpec(memory_space=pl.ANY)] * len(after)
    return pl.pallas_call(
        kernel,
        out_shape=out_shape,
        in_specs=in_specs,
        out_specs=jax.tree.map(lambda _: whole, out_shape),
        scratch_shapes=scratch_shapes,
        compiler_params=pltpu.CompilerParams(vmem_limit_bytes=vmem * MIB),
        cost_estimate=flops and pl.CostEstimate(flops=flops, bytes_accessed=0, transcendentals=0),
    )(*args, *hbm, *after)


def local(inputs, weights, grad_out):
    _, c_dev, planes, cells = inputs.shape
    taps, _, out_all = weights.shape
    n_chan = lax.axis_size("chan")
    n_space = lax.axis_size("space")
    n_batch = lax.axis_size("sample")
    cores = [(i, i ^ 1) for i in range(n_chan)]
    forward = [(i, i + 1) for i in range(n_space - 1)]
    backward = [(target, source) for source, target in forward]
    me = lax.axis_index("chan").reshape(1)
    which = lax.rem(me, 2)
    shape = jax.ShapeDtypeStruct

    plane = shape((c_dev, cells), BF16)

    row, g_planes, x_first, x_second = call(
        send_kernel,
        (
            shape((c_dev, planes * cells + taps * out_all), BF16),
            shape((n_chan, c_dev, cells), BF16),
            plane,
            plane,
        ),
        [
            pltpu.VMEM((c_dev, planes, cells), BF16),
            pltpu.VMEM((c_dev, planes, cells), BF16),
            pltpu.VMEM((taps, c_dev, out_all), BF16),
            pltpu.SemaphoreType.DMA((3,)),
        ],
        hbm=(inputs[0], grad_out[0], weights),
        vmem=60,
    )
    gathered = lax.all_gather(row, "chan", axis=0, tiled=True)
    own = lax.all_to_all(g_planes, "chan", 0, 0).reshape(out_all, cells)
    x_low = lax.ppermute(x_second, "space", forward)
    x_high = lax.ppermute(x_first, "space", backward)
    own, x_low, x_high = lax.optimization_barrier((own, x_low, x_high))
    other = lax.ppermute(own, "chan", cores)

    shares = n_space * n_batch
    x_planes = (x_low, x_first, x_second, x_high)
    first_half = call(
        own_plane_kernel, shape((taps * c_dev, out_all), F32), [], which, *x_planes, own
    )
    partial = call(
        other_plane_kernel,
        shape((shares, c_dev, out_all), F32),
        [],
        which, *x_planes, other, first_half,
    )
    terms = partial
    terms = lax.all_to_all(terms, ("space", "sample"), 0, 0)

    middle, to_below, to_above = call(
        convolve_kernel,
        (
            shape((planes, 2 * c_dev, cells), F32),
            shape((2 * c_dev, cells), F32),
            shape((2 * c_dev, cells), F32),
        ),
        [pltpu.VMEM((planes, taps * c_dev, cells), F32)],
        me, which, gathered, own, other, weights.reshape(taps * c_dev, out_all),
        after=(partial,),
    )
    scale = 1.0 / math.sqrt(shares * planes * cells)
    terms, middle = lax.optimization_barrier((terms, middle))
    spread = call(
        functools.partial(share_kernel, scale), shape(terms.shape, F32), [], terms
    )
    spread, to_above, to_below = lax.optimization_barrier((spread, to_above, to_below))
    shared = lax.all_to_all(spread, ("space", "sample"), 0, 0)
    grad_weights = call(
        take_kernel, shape(weights.shape, F32), [], shared, flops=30_000_000_000
    )

    from_below = lax.ppermute(to_above, "space", forward)
    from_above = lax.ppermute(to_below, "space", backward)
    output, grad_in = call(
        finish_kernel, (shape(inputs.shape[1:], BF16),) * 2, [], middle, from_below, from_above
    )
    return output[None], grad_in[None], grad_weights


def solution(mesh):
    in_specs = (
        P("sample", "chan", "space", None),
        P(None, "chan", None),
        P("sample", "chan", "space", None),
    )
    out_specs = (
        P("sample", "chan", "space", None),
        P("sample", "chan", "space", None),
        P(None, "chan", None),
    )
    return jax.shard_map(local, mesh=mesh, in_specs=in_specs, out_specs=out_specs, check_vma=False)
```

time: 113 us -> 108 us (0.956)
  starting transfers between devices: 42.9 us -> 37.7 us
  Pallas kernels: 11.2 us -> 13.9 us
  local copies, waits for them, and re-layouts: 3.47 us -> 1.68 us
    ppermute x2, waiting for transfers between devices: 1.3 us -> 5.08 us  [the longest x1 4.65 us: local(): x_high = lax.ppermute(x_first, 'space', backward)]
    ppermute x1, starting transfers between devices: 5.35 us -> 1.91 us  [local(): other = lax.ppermute(own, 'chan', cores)]
    all_to_all x1, starting transfers between devices: 14.4 us -> 11.4 us  [local(): terms = lax.all_to_all(terms, ('space', 'sample'), 0, 0)]
    pallas_call x5 -> x7, Pallas kernels: 11.2 us -> 13.9 us  [call(): pl.pallas_call(kernel, out_shape=out_shape, in_specs=in_specs, out_specs=...]
    all_to_all x1, starting transfers between devices: 7.68 us -> 10.3 us  [local(): own = lax.all_to_all(g_planes, 'chan', 0, 0).reshape(out_all, cells)]
    ppermute x2, starting transfers between devices: 5.91 us -> 3.61 us  [the longest x1 2.32 us: local(): x_low = lax.ppermute(x_second, 'space', forward)]
    ppermute x1, waiting for transfers between devices: 2.26 us -> 0.01 us  [local(): other = lax.ppermute(own, 'chan', cores)]
  transfers between devices with their start and end apart: 9 -> 9, of which waited for: 6 -> 6; matrix products, arithmetic and copies ran while one was open for 0% -> 0% of each run, Pallas kernels for 8% -> 9%
where the time goes in v4:
time: 108 us; the launch traced here: 107 us
  waiting for transfers between devices  39.2 us (36%)
  starting transfers between devices  37.7 us (35%)
  between operations  14.2 us (13%)
  Pallas kernels  13.9 us (13%)
  local copies, waits for them, and re-layouts  1.68 us (2%)
    all_to_all x1, waiting for transfers between devices, local(): own = lax.all_to_all(g_planes, 'chan', 0, 0).reshape(out_all, cells)  24.9 us
    pallas_call x7, Pallas kernels, call(): pl.pallas_call(kernel, out_shape=out_shape, in_specs=in_specs, out_specs=...  13.9 us
    all_to_all x1, starting transfers between devices, local(): terms = lax.all_to_all(terms, ('space', 'sample'), 0, 0)  11.4 us
    all_to_all x1, starting transfers between devices, local(): own = lax.all_to_all(g_planes, 'chan', 0, 0).reshape(out_all, cells)  10.3 us
    all_to_all x1, starting transfers between devices, local(): shared = lax.all_to_all(spread, ('space', 'sample'), 0, 0)  5.93 us
    all_to_all x1, waiting for transfers between devices, local(): shared = lax.all_to_all(spread, ('space', 'sample'), 0, 0)  4.89 us
    ppermute x1, waiting for transfers between devices, local(): x_high = lax.ppermute(x_first, 'space', backward)  4.65 us
    all_to_all x1, waiting for transfers between devices, local(): terms = lax.all_to_all(terms, ('space', 'sample'), 0, 0)  3.3 us
  transfers between devices with their start and end apart: 9, of which 6 were waited for; matrix products, arithmetic and copies ran while one was open for 0% of the time, Pallas kernels for 9%

profile of v4, /device:TPU:1, one launch (start us, length us, event | category | flops | bytes accessed | tf_op | source)
XLA Modules:
  0.0 106.6 jit_solution(11667541669930551453)
XLA Ops:
  7.2 0.0 copy-start.2
  7.2 0.0 all-gather.2.cloned.1.call-start
  7.2 2.7 %shard_map.58 = (bf16[8,11648]{1,0:T(8,128)(2,1)}, bf16[16,8,4096]{2,1,0:T(8,128)(2,1)}, bf16[8,4096]{1,0:T(8,128)(2,1)}, bf16[8,4096]{1,0:T(8,128)(2,1)}) custom-call(bf16[8,2,4096]{2,1,0:T(2,128)(2,1)} %bitcast.11, bf16[8,2,4096]{2,1,0:T(2,128)(2,1)} %bitcast.12, bf16[27,8,128]{2,1,0:T(8,128)(2,1)} %w_hbm.1), custom_call_target="tpu_custom_call" | custom-call | tf_op jit(solution)/shard_map/pallas_call | solution.py:182
  9.9 0.0 all-gather.2.cloned.1.call-update
  9.9 10.3 %all-to-all-start = ((bf16[16,8,4096]{2,1,0:T(8,128)(2,1)}), bf16[16,8,4096]{2,1,0:T(8,128)(2,1)S(1)}, u32[]{:S(2)}, u32[]{:S(2)}) async-start(bf16[16,8,4096]{2,1,0:T(8,128)(2,1)} %get-tuple-element.20), calls=%async_computation | async-start | bytes 2097152 | tf_op jit(solution)/shard_map/all_to_all | solution.py:226
  20.3 2.3 %collective-permute-start = (bf16[8,4096]{1,0:T(8,128)(2,1)}, bf16[8,4096]{1,0:T(8,128)(2,1)S(1)}, u32[]{:S(2)}, u32[]{:S(2)}) collective-permute-start(bf16[8,4096]{1,0:T(8,128)(2,1)} %get-tuple-element.21.second_ref), channel_id=1, source_target_pairs={{0,4},{4,8},{8,12},{12,16},{16,20},{20,24},{24,28},{1,5},{5,9},{9,... | collective-permute-start | bytes 196616 | tf_op jit(solution)/shard_map/ppermute | solution.py:227
  22.6 1.3 %collective-permute-start.1 = (bf16[8,4096]{1,0:T(8,128)(2,1)}, bf16[8,4096]{1,0:T(8,128)(2,1)S(1)}, u32[]{:S(2)}, u32[]{:S(2)}) collective-permute-start(bf16[8,4096]{1,0:T(8,128)(2,1)} %get-tuple-element.22.first_ref), channel_id=1, source_target_pairs={{4,0},{8,4},{12,8},{16,12},{20,16},{24,20},{28,24},{5,1},{9,5},{13... | collective-permute-start | bytes 196616 | tf_op jit(solution)/shard_map/ppermute | solution.py:228
  23.9 0.4 collective-permute-done.low_ref
  24.3 4.6 %collective-permute-done.1.high_ref = bf16[8,4096]{1,0:T(8,128)(2,1)S(1)} collective-permute-done((bf16[8,4096]{1,0:T(8,128)(2,1)}, bf16[8,4096]{1,0:T(8,128)(2,1)S(1)}, u32[]{:S(2)}, u32[]{:S(2)}) %collective-permute-start.1) | collective-permute-done | bytes 65568 | tf_op jit(solution)/shard_map/ppermute | solution.py:228
  29.0 24.9 %all-to-all-done = bf16[16,8,4096]{2,1,0:T(8,128)(2,1)S(1)} async-done(((bf16[16,8,4096]{2,1,0:T(8,128)(2,1)}), bf16[16,8,4096]{2,1,0:T(8,128)(2,1)S(1)}, u32[]{:S(2)}, u32[]{:S(2)}) %all-to-all-start) | async-done | bytes 1048608 | tf_op jit(solution)/shard_map/all_to_all | solution.py:226
  53.9 1.9 %collective-permute-start.2 = (bf16[128,4096]{1,0:T(8,128)(2,1)S(1)}, bf16[128,4096]{1,0:T(8,128)(2,1)S(1)}, u32[]{:S(2)}, u32[]{:S(2)}) collective-permute-start(bf16[128,4096]{1,0:T(8,128)(2,1)S(1)} %bitcast.7), channel_id=1, source_target_pairs={{0,32},{32,0},{64,96},{96,64},{128,160},{160,128},{192,224},{224,1... | collective-permute-start | bytes 3145736 | tf_op jit(solution)/shard_map/ppermute | solution.py:230
  55.8 0.0 copy-start
  55.8 0.8 copy-done
  56.6 0.0 copy-start.1
  56.7 0.8 copy-done.1
  57.5 1.1 shard_map.59.own_ref
  58.6 0.0 collective-permute-done.2.g_ref.other_ref
  58.6 1.8 %shard_map.60.after_ref = f32[32,8,128]{2,1,0:T(8,128)} custom-call(s32[1]{0:T(128)S(6)} %rem.18.which_ref, bf16[8,4096]{1,0:T(8,128)(2,1)S(1)} %collective-permute-done.low_ref, bf16[8,4096]{1,0:T(8,128)(2,1)S(1)} %copy-done, bf16[8,4096]{1,0:T(8,128)(2,1)S(1)} %copy-done.1, bf16[8,4096]{1,0:T(8,128)(2,1)S(1)} %collective-permute-done.1.high_ref, ...), custom_call_target="tpu_custom_call" | custom-call | tf_op jit(solution)/shard_map/pallas_call | solution.py:182
  60.3 11.4 %all-to-all-start.1 = ((f32[32,8,128]{2,1,0:T(8,128)}), f32[32,8,128]{2,1,0:T(8,128)S(1)}, u32[]{:S(2)}, u32[]{:S(2)}) async-start(f32[32,8,128]{2,1,0:T(8,128)} %shard_map.60.after_ref), calls=%async_computation.1 | async-start | bytes 262144 | tf_op jit(solution)/shard_map/all_to_all | solution.py:244
  71.7 0.0 all-gather.2.cloned.1.call-done.all_ref
  71.8 0.0 copy-done.2
  71.8 6.0 %shard_map.61 = (f32[2,16,4096]{2,1,0:T(8,128)S(1)}, f32[16,4096]{1,0:T(8,128)S(1)}, f32[16,4096]{1,0:T(8,128)S(1)}) custom-call(s32[1]{0:T(128)} %bitcast.me_ref, s32[1]{0:T(128)S(6)} %rem.18.which_ref, bf16[128,11648]{1,0:T(8,128)(2,1)} %all-gather.2.cloned.1.call-done.all_ref, bf16[128,4096]{1,0:T(8,128)(2,1)S(1)} %bitcast.9, ...), custom_call_target="tpu_custom_call" | custom-call | tf_op jit(solution)/shard_map/pallas_call | solution.py:182
  77.8 3.3 %all-to-all-done.1.terms_ref = f32[32,8,128]{2,1,0:T(8,128)S(1)} async-done(((f32[32,8,128]{2,1,0:T(8,128)}), f32[32,8,128]{2,1,0:T(8,128)S(1)}, u32[]{:S(2)}, u32[]{:S(2)}) %all-to-all-start.1) | async-done | bytes 131104 | tf_op jit(solution)/shard_map/all_to_all | solution.py:244
  81.1 0.7 shard_map.62
  81.8 5.9 %all-to-all-start.2 = ((f32[32,8,128]{2,1,0:T(8,128)}), f32[32,8,128]{2,1,0:T(8,128)S(1)}, u32[]{:S(2)}, u32[]{:S(2)}) async-start(f32[32,8,128]{2,1,0:T(8,128)} %shard_map.62), calls=%async_computation.2 | async-start | bytes 262144 | tf_op jit(solution)/shard_map/all_to_all | solution.py:263
  87.7 3.2 %collective-permute-start.3 = (f32[16,4096]{1,0:T(8,128)S(1)}, f32[16,4096]{1,0:T(8,128)S(1)}, u32[]{:S(2)}, u32[]{:S(2)}) collective-permute-start(f32[16,4096]{1,0:T(8,128)S(1)} %get-tuple-element.32), channel_id=1, source_target_pairs={{0,4},{4,8},{8,12},{12,16},{16,20},{20,24},{24,28},{1,5},{5,9},{9,... | collective-permute-start | bytes 786440 | tf_op jit(solution)/shard_map/ppermute | solution.py:268
  90.9 1.3 %collective-permute-start.4 = (f32[16,4096]{1,0:T(8,128)S(1)}, f32[16,4096]{1,0:T(8,128)S(1)}, u32[]{:S(2)}, u32[]{:S(2)}) collective-permute-start(f32[16,4096]{1,0:T(8,128)S(1)} %get-tuple-element.33), channel_id=1, source_target_pairs={{4,0},{8,4},{12,8},{16,12},{20,16},{24,20},{28,24},{5,1},{9,5},{13... | collective-permute-start | bytes 786440 | tf_op jit(solution)/shard_map/ppermute | solution.py:269
  92.2 4.9 %all-to-all-done.2.shares_ref = f32[32,8,128]{2,1,0:T(8,128)S(1)} async-done(((f32[32,8,128]{2,1,0:T(8,128)}), f32[32,8,128]{2,1,0:T(8,128)S(1)}, u32[]{:S(2)}, u32[]{:S(2)}) %all-to-all-start.2) | async-done | bytes 131104 | tf_op jit(solution)/shard_map/all_to_all | solution.py:263
  97.1 0.7 shard_map.64
  97.7 0.0 collective-permute-done.3.below_ref
  97.7 0.9 collective-permute-done.4.above_ref
  98.6 1.1 %shard_map.63 = (bf16[8,2,4096]{2,1,0:T(2,128)(2,1)}, bf16[8,2,4096]{2,1,0:T(2,128)(2,1)}) custom-call(f32[2,16,4096]{2,1,0:T(8,128)S(1)} %get-tuple-element.28.middle_ref, f32[16,4096]{1,0:T(8,128)S(1)} %collective-permute-done.3.below_ref, f32[16,4096]{1,0:T(8,128)S(1)} %collective-permute-done.4.above_ref), custom_call_target="tpu_custom_call" | custom-call | tf_op jit(solution)/shard_map/pallas_call | solution.py:182
Async XLA Ops:
  7.2 64.6 %copy-start.2 = (bf16[27,8,128]{2,1,0:T(8,128)(2,1)S(1)}, bf16[27,8,128]{2,1,0:T(8,128)(2,1)}, u32[]{:S(2)}) copy-start(bf16[27,8,128]{2,1,0:T(8,128)(2,1)} %w_hbm.1) | copy-start | bytes 165892
  7.2 64.6 %all-gather.2.cloned.1.call-start = ((), (), s32[]{:S(2)}) async-start(), calls=%async_computation.3 | async-start | bytes 3168256 | tf_op jit(solution)/shard_map/all_gather | solution.py:225
  9.9 43.9 %all-to-all-start = ((bf16[16,8,4096]{2,1,0:T(8,128)(2,1)}), bf16[16,8,4096]{2,1,0:T(8,128)(2,1)S(1)}, u32[]{:S(2)}, u32[]{:S(2)}) async-start(bf16[16,8,4096]{2,1,0:T(8,128)(2,1)} %get-tuple-element.20), calls=%async_computation | async-start | bytes 2097152 | tf_op jit(solution)/shard_map/all_to_all | solution.py:226
  20.3 4.1 %collective-permute-start = (bf16[8,4096]{1,0:T(8,128)(2,1)}, bf16[8,4096]{1,0:T(8,128)(2,1)S(1)}, u32[]{:S(2)}, u32[]{:S(2)}) collective-permute-start(bf16[8,4096]{1,0:T(8,128)(2,1)} %get-tuple-element.21.second_ref), channel_id=1, source_target_pairs={{0,4},{4,8},{8,12},{12,16},{16,20},{20,24},{24,28},{1,5},{5,9},{9,... | collective-permute-start | bytes 196616 | tf_op jit(solution)/shard_map/ppermute | solution.py:227
  22.6 6.4 %collective-permute-start.1 = (bf16[8,4096]{1,0:T(8,128)(2,1)}, bf16[8,4096]{1,0:T(8,128)(2,1)S(1)}, u32[]{:S(2)}, u32[]{:S(2)}) collective-permute-start(bf16[8,4096]{1,0:T(8,128)(2,1)} %get-tuple-element.22.first_ref), channel_id=1, source_target_pairs={{4,0},{8,4},{12,8},{16,12},{20,16},{24,20},{28,24},{5,1},{9,5},{13... | collective-permute-start | bytes 196616 | tf_op jit(solution)/shard_map/ppermute | solution.py:228
  53.9 4.7 %collective-permute-start.2 = (bf16[128,4096]{1,0:T(8,128)(2,1)S(1)}, bf16[128,4096]{1,0:T(8,128)(2,1)S(1)}, u32[]{:S(2)}, u32[]{:S(2)}) collective-permute-start(bf16[128,4096]{1,0:T(8,128)(2,1)S(1)} %bitcast.7), channel_id=1, source_target_pairs={{0,32},{32,0},{64,96},{96,64},{128,160},{160,128},{192,224},{224,1... | collective-permute-start | bytes 3145736 | tf_op jit(solution)/shard_map/ppermute | solution.py:230
  55.8 0.8 copy-start
  56.6 0.8 copy-start.1
  60.3 20.8 %all-to-all-start.1 = ((f32[32,8,128]{2,1,0:T(8,128)}), f32[32,8,128]{2,1,0:T(8,128)S(1)}, u32[]{:S(2)}, u32[]{:S(2)}) async-start(f32[32,8,128]{2,1,0:T(8,128)} %shard_map.60.after_ref), calls=%async_computation.1 | async-start | bytes 262144 | tf_op jit(solution)/shard_map/all_to_all | solution.py:244
  81.8 15.3 %all-to-all-start.2 = ((f32[32,8,128]{2,1,0:T(8,128)}), f32[32,8,128]{2,1,0:T(8,128)S(1)}, u32[]{:S(2)}, u32[]{:S(2)}) async-start(f32[32,8,128]{2,1,0:T(8,128)} %shard_map.62), calls=%async_computation.2 | async-start | bytes 262144 | tf_op jit(solution)/shard_map/all_to_all | solution.py:263
  87.7 10.0 %collective-permute-start.3 = (f32[16,4096]{1,0:T(8,128)S(1)}, f32[16,4096]{1,0:T(8,128)S(1)}, u32[]{:S(2)}, u32[]{:S(2)}) collective-permute-start(f32[16,4096]{1,0:T(8,128)S(1)} %get-tuple-element.32), channel_id=1, source_target_pairs={{0,4},{4,8},{8,12},{12,16},{16,20},{20,24},{24,28},{1,5},{5,9},{9,... | collective-permute-start | bytes 786440 | tf_op jit(solution)/shard_map/ppermute | solution.py:268
  90.9 7.8 %collective-permute-start.4 = (f32[16,4096]{1,0:T(8,128)S(1)}, f32[16,4096]{1,0:T(8,128)S(1)}, u32[]{:S(2)}, u32[]{:S(2)}) collective-permute-start(f32[16,4096]{1,0:T(8,128)S(1)} %get-tuple-element.33), channel_id=1, source_target_pairs={{4,0},{8,4},{12,8},{16,12},{20,16},{24,20},{28,24},{5,1},{9,5},{13... | collective-permute-start | bytes 786440 | tf_op jit(solution)/shard_map/ppermute | solution.py:269
Sparse Core Ops, SparseCore 0:
  10.1 58.5 all-gather.1

commit v5 on v4

--- a/solution.py
+++ b/solution.py
@@ -65,34 +65,33 @@
         row_ref[:, start : start + out_all] = w_ref[tap]
 
 
-def kernel_grad(plane, planes, g_ref):
-    moved = []
-    for plane_k in range(3):
-        wide = jnp.where(
-            plane == 0, planes[plane_k][...].astype(F32), planes[plane_k + 1][...].astype(F32)
-        )
-        for rows in (-1, 0, 1):
-            turned = shift_rows(wide, rows) if rows else wide
-            for cols in (-1, 0, 1):
-                moved.append(shift_cols(turned, cols) if cols else turned)
+def columns_kernel(which_ref, low_ref, first_ref, second_ref, high_ref, own_ref, other_ref):
+    planes = (low_ref, first_ref, second_ref, high_ref)
+    for out_ref, plane in ((own_ref, which_ref[0]), (other_ref, 1 - which_ref[0])):
+        moved = []
+        for plane_k in range(3):
+            wide = jnp.where(
+                plane == 0, planes[plane_k][...].astype(F32), planes[plane_k + 1][...].astype(F32)
+            )
+            for rows in (-1, 0, 1):
+                turned = shift_rows(wide, rows) if rows else wide
+                for cols in (-1, 0, 1):
+                    moved.append(shift_cols(turned, cols) if cols else turned)
+        out_ref[...] = jnp.concatenate(moved, axis=0).astype(BF16)
+
+
+def kernel_grad(columns_ref, g_ref):
     return lax.dot_general(
-        jnp.concatenate(moved, axis=0).astype(BF16),
-        g_ref[...],
-        (((1,), (1,)), ((), ())),
-        preferred_element_type=F32,
-    )
-
-
-def own_plane_kernel(which_ref, low_ref, first_ref, second_ref, high_ref, g_ref, out_ref):
-    planes = (low_ref, first_ref, second_ref, high_ref)
-    out_ref[...] = kernel_grad(which_ref[0], planes, g_ref)
-
-
-def other_plane_kernel(
-    which_ref, low_ref, first_ref, second_ref, high_ref, g_ref, own_ref, out_ref
-):
-    planes = (low_ref, first_ref, second_ref, high_ref)
-    total = own_ref[...] + kernel_grad(1 - which_ref[0], planes, g_ref)
+        columns_ref[...], g_ref[...], (((1,), (1,)), ((), ())), preferred_element_type=F32
+    )
+
+
+def own_plane_kernel(columns_ref, g_ref, out_ref):
+    out_ref[...] = kernel_grad(columns_ref, g_ref)
+
+
+def other_plane_kernel(columns_ref, g_ref, own_ref, out_ref):
+    total = own_ref[...] + kernel_grad(columns_ref, g_ref)
     c_rows = out_ref.shape[1]
     for tap in range(27):
         out_ref[tap] = total[tap * c_rows : (tap + 1) * c_rows]
@@ -226,19 +225,22 @@
     own = lax.all_to_all(g_planes, "chan", 0, 0).reshape(out_all, cells)
     x_low = lax.ppermute(x_second, "space", forward)
     x_high = lax.ppermute(x_first, "space", backward)
-    own, x_low, x_high = lax.optimization_barrier((own, x_low, x_high))
+    columns = shape((taps * c_dev, cells), BF16)
+    own_columns, other_columns = call(
+        columns_kernel, (columns, columns), [], which, x_low, x_first, x_second, x_high
+    )
+    own, own_columns, other_columns = lax.optimization_barrier((own, own_columns, other_columns))
     other = lax.ppermute(own, "chan", cores)
 
     shares = n_space * n_batch
-    x_planes = (x_low, x_first, x_second, x_high)
     first_half = call(
-        own_plane_kernel, shape((taps * c_dev, out_all), F32), [], which, *x_planes, own
+        own_plane_kernel, shape((taps * c_dev, out_all), F32), [], own_columns, own
     )
     partial = call(
         other_plane_kernel,
         shape((shares, c_dev, out_all), F32),
         [],
-        which, *x_planes, other, first_half,
+        other_columns, other, first_half,
     )
     terms = partial
     terms = lax.all_to_all(terms, ("space", "sample"), 0, 0)

time: 108 us -> 108 us (level)
  waiting for transfers between devices: 39.2 us -> 36.7 us
  local copies, waits for them, and re-layouts: 1.68 us -> 4.05 us
    all_to_all x1, waiting for transfers between devices: 24.9 us -> 21.3 us  [local(): own = lax.all_to_all(g_planes, 'chan', 0, 0).reshape(out_all, cells)]
    unnamed x6 -> x14, local copies, waits for them, and re-layouts: 1.68 us -> 4.05 us
    pallas_call x7 -> x8, Pallas kernels: 13.9 us -> 14.3 us  [call(): pl.pallas_call(kernel, out_shape=out_shape, in_specs=in_specs, out_specs=...]
where the time goes in v5:
time: 108 us; the launch traced here: 107 us
  starting transfers between devices  37.6 us (35%)
  waiting for transfers between devices  36.7 us (34%)
  Pallas kernels  14.3 us (13%)
  between operations  14.2 us (13%)
  local copies, waits for them, and re-layouts  4.05 us (4%)
    all_to_all x1, waiting for transfers between devices, local(): own = lax.all_to_all(g_planes, 'chan', 0, 0).reshape(out_all, cells)  21.3 us
    pallas_call x8, Pallas kernels, call(): pl.pallas_call(kernel, out_shape=out_shape, in_specs=in_specs, out_specs=...  14.3 us
    all_to_all x1, starting transfers between devices, local(): terms = lax.all_to_all(terms, ('space', 'sample'), 0, 0)  11.6 us
    all_to_all x1, starting transfers between devices, local(): own = lax.all_to_all(g_planes, 'chan', 0, 0).reshape(out_all, cells)  10.5 us
    all_to_all x1, starting transfers between devices, local(): shared = lax.all_to_all(spread, ('space', 'sample'), 0, 0)  5.41 us
    all_to_all x1, waiting for transfers between devices, local(): shared = lax.all_to_all(spread, ('space', 'sample'), 0, 0)  4.89 us
    ppermute x1, waiting for transfers between devices, local(): x_high = lax.ppermute(x_first, 'space', backward)  4.85 us
    unnamed x14, local copies, waits for them, and re-layouts  4.05 us
  transfers between devices with their start and end apart: 9, of which 6 were waited for; matrix products, arithmetic and copies ran while one was open for 0% of the time, Pallas kernels for 9%

profile of v5, /device:TPU:1, one launch (start us, length us, event | category | flops | bytes accessed | tf_op | source)
XLA Modules:
  0.0 106.8 jit_solution(194380586195317568)
XLA Ops:
  7.2 0.0 all-gather.2.cloned.1.call-start
  7.2 2.7 %shard_map.58 = (bf16[8,11648]{1,0:T(8,128)(2,1)}, bf16[16,8,4096]{2,1,0:T(8,128)(2,1)}, bf16[8,4096]{1,0:T(8,128)(2,1)}, bf16[8,4096]{1,0:T(8,128)(2,1)}) custom-call(bf16[8,2,4096]{2,1,0:T(2,128)(2,1)} %bitcast.11, bf16[8,2,4096]{2,1,0:T(2,128)(2,1)} %bitcast.12, bf16[27,8,128]{2,1,0:T(8,128)(2,1)} %w_hbm.1), custom_call_target="tpu_custom_call" | custom-call | tf_op jit(solution)/shard_map/pallas_call | solution.py:181
  9.9 0.0 copy-start.6
  9.9 0.0 copy-start.5
  9.9 0.0 all-gather.2.cloned.1.call-update
  10.0 10.5 %all-to-all-start = ((bf16[16,8,4096]{2,1,0:T(8,128)(2,1)}), bf16[16,8,4096]{2,1,0:T(8,128)(2,1)S(1)}, u32[]{:S(2)}, u32[]{:S(2)}) async-start(bf16[16,8,4096]{2,1,0:T(8,128)(2,1)} %get-tuple-element.22), calls=%async_computation | async-start | bytes 2097152 | tf_op jit(solution)/shard_map/all_to_all | solution.py:225
  20.4 0.0 copy-done.6
  20.4 2.3 %collective-permute-start = (bf16[8,4096]{1,0:T(8,128)(2,1)S(1)}, bf16[8,4096]{1,0:T(8,128)(2,1)S(1)}, u32[]{:S(2)}, u32[]{:S(2)}) collective-permute-start(bf16[8,4096]{1,0:T(8,128)(2,1)S(1)} %copy-done.6), channel_id=1, source_target_pairs={{0,4},{4,8},{8,12},{12,16},{16,20},{20,24},{24,28},{1,5},{5,9},{9,... | collective-permute-start | bytes 196616 | tf_op jit(solution)/shard_map/ppermute | solution.py:226
  22.7 0.0 copy-done.5
  22.8 1.3 %collective-permute-start.1 = (bf16[8,4096]{1,0:T(8,128)(2,1)S(1)}, bf16[8,4096]{1,0:T(8,128)(2,1)S(1)}, u32[]{:S(2)}, u32[]{:S(2)}) collective-permute-start(bf16[8,4096]{1,0:T(8,128)(2,1)S(1)} %copy-done.5), channel_id=1, source_target_pairs={{4,0},{8,4},{12,8},{16,12},{20,16},{24,20},{28,24},{5,1},{9,5},{13... | collective-permute-start | bytes 196616 | tf_op jit(solution)/shard_map/ppermute | solution.py:227
  24.1 0.0 collective-permute-done.low_ref
  24.1 4.9 %collective-permute-done.1.high_ref = bf16[8,4096]{1,0:T(8,128)(2,1)S(1)} collective-permute-done((bf16[8,4096]{1,0:T(8,128)(2,1)S(1)}, bf16[8,4096]{1,0:T(8,128)(2,1)S(1)}, u32[]{:S(2)}, u32[]{:S(2)}) %collective-permute-start.1) | collective-permute-done | bytes 65568 | tf_op jit(solution)/shard_map/ppermute | solution.py:227
  28.9 1.3 %shard_map.59 = (bf16[216,4096]{1,0:T(8,128)(2,1)S(1)}, bf16[216,4096]{1,0:T(8,128)(2,1)S(1)}) custom-call(s32[1]{0:T(128)S(6)} %rem.18.which_ref, bf16[8,4096]{1,0:T(8,128)(2,1)S(1)} %collective-permute-done.low_ref, bf16[8,4096]{1,0:T(8,128)(2,1)S(1)} %copy-done.5, bf16[8,4096]{1,0:T(8,128)(2,1)S(1)} %copy-done.6, ...), custom_call_target="tpu_custom_call" | custom-call | tf_op jit(solution)/shard_map/pallas_call | solution.py:181
  30.2 0.0 copy-start
  30.2 1.3 %copy-done = bf16[216,4096]{1,0:T(8,128)(2,1)} copy-done((bf16[216,4096]{1,0:T(8,128)(2,1)}, bf16[216,4096]{1,0:T(8,128)(2,1)S(1)}, u32[]{:S(2)}) %copy-start) | copy-done | bytes 1769496
  31.4 0.0 copy-start.2
  31.5 1.3 %copy-done.2 = bf16[216,4096]{1,0:T(8,128)(2,1)} copy-done((bf16[216,4096]{1,0:T(8,128)(2,1)}, bf16[216,4096]{1,0:T(8,128)(2,1)S(1)}, u32[]{:S(2)}) %copy-start.2) | copy-done | bytes 1769496
  32.7 21.3 %all-to-all-done = bf16[16,8,4096]{2,1,0:T(8,128)(2,1)S(1)} async-done(((bf16[16,8,4096]{2,1,0:T(8,128)(2,1)}), bf16[16,8,4096]{2,1,0:T(8,128)(2,1)S(1)}, u32[]{:S(2)}, u32[]{:S(2)}) %all-to-all-start) | async-done | bytes 1048608 | tf_op jit(solution)/shard_map/all_to_all | solution.py:225
  54.0 0.0 copy-start.1
  54.0 2.0 %collective-permute-start.2 = (bf16[128,4096]{1,0:T(8,128)(2,1)S(1)}, bf16[128,4096]{1,0:T(8,128)(2,1)S(1)}, u32[]{:S(2)}, u32[]{:S(2)}) collective-permute-start(bf16[128,4096]{1,0:T(8,128)(2,1)S(1)} %bitcast.7), channel_id=1, source_target_pairs={{0,32},{32,0},{64,96},{96,64},{128,160},{160,128},{192,224},{224,1... | collective-permute-start | bytes 3145736 | tf_op jit(solution)/shard_map/ppermute | solution.py:233
  56.1 0.0 copy-start.3
  56.1 1.5 %copy-done.3 = bf16[216,4096]{1,0:T(8,128)(2,1)S(1)} copy-done((bf16[216,4096]{1,0:T(8,128)(2,1)S(1)}, bf16[216,4096]{1,0:T(8,128)(2,1)}, u32[]{:S(2)}) %copy-start.3) | copy-done | bytes 1769496
  57.6 0.6 shard_map.60.own_ref
  58.2 0.0 copy-start.4
  58.2 0.5 collective-permute-done.2.g_ref.other_ref
  58.7 0.0 copy-done.1
  58.7 1.3 %shard_map.61.after_ref = f32[32,8,128]{2,1,0:T(8,128)} custom-call(bf16[216,4096]{1,0:T(8,128)(2,1)S(1)} %copy-done.1, bf16[128,4096]{1,0:T(8,128)(2,1)S(1)} %collective-permute-done.2.g_ref.other_ref, f32[216,128]{1,0:T(8,128)S(1)} %shard_map.60.own_ref), custom_call_target="tpu_custom_call" | custom-call | tf_op jit(solution)/shard_map/pallas_call | solution.py:181
  60.0 11.6 %all-to-all-start.1 = ((f32[32,8,128]{2,1,0:T(8,128)}), f32[32,8,128]{2,1,0:T(8,128)S(1)}, u32[]{:S(2)}, u32[]{:S(2)}) async-start(f32[32,8,128]{2,1,0:T(8,128)} %shard_map.61.after_ref), calls=%async_computation.1 | async-start | bytes 262144 | tf_op jit(solution)/shard_map/all_to_all | solution.py:246
  71.6 0.0 all-gather.2.cloned.1.call-done.all_ref
  71.6 0.0 copy-done.4
  71.7 6.0 %shard_map.62 = (f32[2,16,4096]{2,1,0:T(8,128)S(1)}, f32[16,4096]{1,0:T(8,128)S(1)}, f32[16,4096]{1,0:T(8,128)S(1)}) custom-call(s32[1]{0:T(128)} %bitcast.3.me_ref, s32[1]{0:T(128)S(6)} %rem.18.which_ref, bf16[128,11648]{1,0:T(8,128)(2,1)} %all-gather.2.cloned.1.call-done.all_ref, bf16[128,4096]{1,0:T(8,128)(2,1)S(1)} %bitcast.9, ...), custom_call_target="tpu_custom_call" | custom-call | tf_op jit(solution)/shard_map/pallas_call | solution.py:181
  77.6 3.8 %all-to-all-done.1.terms_ref = f32[32,8,128]{2,1,0:T(8,128)S(1)} async-done(((f32[32,8,128]{2,1,0:T(8,128)}), f32[32,8,128]{2,1,0:T(8,128)S(1)}, u32[]{:S(2)}, u32[]{:S(2)}) %all-to-all-start.1) | async-done | bytes 131104 | tf_op jit(solution)/shard_map/all_to_all | solution.py:246
  81.4 0.7 shard_map.63
  82.1 5.4 %all-to-all-start.2 = ((f32[32,8,128]{2,1,0:T(8,128)}), f32[32,8,128]{2,1,0:T(8,128)S(1)}, u32[]{:S(2)}, u32[]{:S(2)}) async-start(f32[32,8,128]{2,1,0:T(8,128)} %shard_map.63), calls=%async_computation.2 | async-start | bytes 262144 | tf_op jit(solution)/shard_map/all_to_all | solution.py:265
  87.6 3.2 %collective-permute-start.3 = (f32[16,4096]{1,0:T(8,128)S(1)}, f32[16,4096]{1,0:T(8,128)S(1)}, u32[]{:S(2)}, u32[]{:S(2)}) collective-permute-start(f32[16,4096]{1,0:T(8,128)S(1)} %get-tuple-element.36), channel_id=1, source_target_pairs={{0,4},{4,8},{8,12},{12,16},{16,20},{20,24},{24,28},{1,5},{5,9},{9,... | collective-permute-start | bytes 786440 | tf_op jit(solution)/shard_map/ppermute | solution.py:270
  90.7 1.3 %collective-permute-start.4 = (f32[16,4096]{1,0:T(8,128)S(1)}, f32[16,4096]{1,0:T(8,128)S(1)}, u32[]{:S(2)}, u32[]{:S(2)}) collective-permute-start(f32[16,4096]{1,0:T(8,128)S(1)} %get-tuple-element.37), channel_id=1, source_target_pairs={{4,0},{8,4},{12,8},{16,12},{20,16},{24,20},{28,24},{5,1},{9,5},{13... | collective-permute-start | bytes 786440 | tf_op jit(solution)/shard_map/ppermute | solution.py:271
  92.0 4.9 %all-to-all-done.2.shares_ref = f32[32,8,128]{2,1,0:T(8,128)S(1)} async-done(((f32[32,8,128]{2,1,0:T(8,128)}), f32[32,8,128]{2,1,0:T(8,128)S(1)}, u32[]{:S(2)}, u32[]{:S(2)}) %all-to-all-start.2) | async-done | bytes 131104 | tf_op jit(solution)/shard_map/all_to_all | solution.py:265
  96.9 0.7 shard_map.65
  97.6 0.0 collective-permute-done.3.below_ref
  97.6 1.3 %collective-permute-done.4.above_ref = f32[16,4096]{1,0:T(8,128)S(1)} collective-permute-done((f32[16,4096]{1,0:T(8,128)S(1)}, f32[16,4096]{1,0:T(8,128)S(1)}, u32[]{:S(2)}, u32[]{:S(2)}) %collective-permute-start.4) | collective-permute-done | bytes 262176 | tf_op jit(solution)/shard_map/ppermute | solution.py:271
  98.9 1.1 %shard_map.64 = (bf16[8,2,4096]{2,1,0:T(2,128)(2,1)}, bf16[8,2,4096]{2,1,0:T(2,128)(2,1)}) custom-call(f32[2,16,4096]{2,1,0:T(8,128)S(1)} %get-tuple-element.32.middle_ref, f32[16,4096]{1,0:T(8,128)S(1)} %collective-permute-done.3.below_ref, f32[16,4096]{1,0:T(8,128)S(1)} %collective-permute-done.4.above_ref), custom_call_target="tpu_custom_call" | custom-call | tf_op jit(solution)/shard_map/pallas_call | solution.py:181
Async XLA Ops:
  7.2 64.5 %all-gather.2.cloned.1.call-start = ((), (), s32[]{:S(2)}) async-start(), calls=%async_computation.3 | async-start | bytes 3168256 | tf_op jit(solution)/shard_map/all_gather | solution.py:224
  9.9 10.5 %copy-start.6 = (bf16[8,4096]{1,0:T(8,128)(2,1)S(1)}, bf16[8,4096]{1,0:T(8,128)(2,1)}, u32[]{:S(2)}) copy-start(bf16[8,4096]{1,0:T(8,128)(2,1)} %get-tuple-element.23.second_ref) | copy-start | bytes 196612
  9.9 12.8 %copy-start.5 = (bf16[8,4096]{1,0:T(8,128)(2,1)S(1)}, bf16[8,4096]{1,0:T(8,128)(2,1)}, u32[]{:S(2)}) copy-start(bf16[8,4096]{1,0:T(8,128)(2,1)} %get-tuple-element.24.first_ref) | copy-start | bytes 196612
  10.0 44.1 %all-to-all-start = ((bf16[16,8,4096]{2,1,0:T(8,128)(2,1)}), bf16[16,8,4096]{2,1,0:T(8,128)(2,1)S(1)}, u32[]{:S(2)}, u32[]{:S(2)}) async-start(bf16[16,8,4096]{2,1,0:T(8,128)(2,1)} %get-tuple-element.22), calls=%async_computation | async-start | bytes 2097152 | tf_op jit(solution)/shard_map/all_to_all | solution.py:225
  20.4 3.6 %collective-permute-start = (bf16[8,4096]{1,0:T(8,128)(2,1)S(1)}, bf16[8,4096]{1,0:T(8,128)(2,1)S(1)}, u32[]{:S(2)}, u32[]{:S(2)}) collective-permute-start(bf16[8,4096]{1,0:T(8,128)(2,1)S(1)} %copy-done.6), channel_id=1, source_target_pairs={{0,4},{4,8},{8,12},{12,16},{16,20},{20,24},{24,28},{1,5},{5,9},{9,... | collective-permute-start | bytes 196616 | tf_op jit(solution)/shard_map/ppermute | solution.py:226
  22.8 6.2 %collective-permute-start.1 = (bf16[8,4096]{1,0:T(8,128)(2,1)S(1)}, bf16[8,4096]{1,0:T(8,128)(2,1)S(1)}, u32[]{:S(2)}, u32[]{:S(2)}) collective-permute-start(bf16[8,4096]{1,0:T(8,128)(2,1)S(1)} %copy-done.5), channel_id=1, source_target_pairs={{4,0},{8,4},{12,8},{16,12},{20,16},{24,20},{28,24},{5,1},{9,5},{13... | collective-permute-start | bytes 196616 | tf_op jit(solution)/shard_map/ppermute | solution.py:227
  30.2 1.3 %copy-start = (bf16[216,4096]{1,0:T(8,128)(2,1)}, bf16[216,4096]{1,0:T(8,128)(2,1)S(1)}, u32[]{:S(2)}) copy-start(bf16[216,4096]{1,0:T(8,128)(2,1)S(1)} %get-tuple-element.27.columns_ref) | copy-start | bytes 5308420
  31.4 1.3 %copy-start.2 = (bf16[216,4096]{1,0:T(8,128)(2,1)}, bf16[216,4096]{1,0:T(8,128)(2,1)S(1)}, u32[]{:S(2)}) copy-start(bf16[216,4096]{1,0:T(8,128)(2,1)S(1)} %get-tuple-element.29.columns_ref) | copy-start | bytes 5308420
  54.0 4.7 %copy-start.1 = (bf16[216,4096]{1,0:T(8,128)(2,1)S(1)}, bf16[216,4096]{1,0:T(8,128)(2,1)}, u32[]{:S(2)}) copy-start(bf16[216,4096]{1,0:T(8,128)(2,1)} %copy-done) | copy-start | bytes 5308420
  54.0 4.7 %collective-permute-start.2 = (bf16[128,4096]{1,0:T(8,128)(2,1)S(1)}, bf16[128,4096]{1,0:T(8,128)(2,1)S(1)}, u32[]{:S(2)}, u32[]{:S(2)}) collective-permute-start(bf16[128,4096]{1,0:T(8,128)(2,1)S(1)} %bitcast.7), channel_id=1, source_target_pairs={{0,32},{32,0},{64,96},{96,64},{128,160},{160,128},{192,224},{224,1... | collective-permute-start | bytes 3145736 | tf_op jit(solution)/shard_map/ppermute | solution.py:233
  56.1 1.5 %copy-start.3 = (bf16[216,4096]{1,0:T(8,128)(2,1)S(1)}, bf16[216,4096]{1,0:T(8,128)(2,1)}, u32[]{:S(2)}) copy-start(bf16[216,4096]{1,0:T(8,128)(2,1)} %copy-done.2) | copy-start | bytes 5308420
  58.2 13.4 %copy-start.4 = (bf16[27,8,128]{2,1,0:T(8,128)(2,1)S(1)}, bf16[27,8,128]{2,1,0:T(8,128)(2,1)}, u32[]{:S(2)}) copy-start(bf16[27,8,128]{2,1,0:T(8,128)(2,1)} %w_hbm.1) | copy-start | bytes 165892
  60.0 21.4 %all-to-all-start.1 = ((f32[32,8,128]{2,1,0:T(8,128)}), f32[32,8,128]{2,1,0:T(8,128)S(1)}, u32[]{:S(2)}, u32[]{:S(2)}) async-start(f32[32,8,128]{2,1,0:T(8,128)} %shard_map.61.after_ref), calls=%async_computation.1 | async-start | bytes 262144 | tf_op jit(solution)/shard_map/all_to_all | solution.py:246
  82.1 14.8 %all-to-all-start.2 = ((f32[32,8,128]{2,1,0:T(8,128)}), f32[32,8,128]{2,1,0:T(8,128)S(1)}, u32[]{:S(2)}, u32[]{:S(2)}) async-start(f32[32,8,128]{2,1,0:T(8,128)} %shard_map.63), calls=%async_computation.2 | async-start | bytes 262144 | tf_op jit(solution)/shard_map/all_to_all | solution.py:265
  87.6 10.0 %collective-permute-start.3 = (f32[16,4096]{1,0:T(8,128)S(1)}, f32[16,4096]{1,0:T(8,128)S(1)}, u32[]{:S(2)}, u32[]{:S(2)}) collective-permute-start(f32[16,4096]{1,0:T(8,128)S(1)} %get-tuple-element.36), channel_id=1, source_target_pairs={{0,4},{4,8},{8,12},{12,16},{16,20},{20,24},{24,28},{1,5},{5,9},{9,... | collective-permute-start | bytes 786440 | tf_op jit(solution)/shard_map/ppermute | solution.py:270
  90.7 8.1 %collective-permute-start.4 = (f32[16,4096]{1,0:T(8,128)S(1)}, f32[16,4096]{1,0:T(8,128)S(1)}, u32[]{:S(2)}, u32[]{:S(2)}) collective-permute-start(f32[16,4096]{1,0:T(8,128)S(1)} %get-tuple-element.37), channel_id=1, source_target_pairs={{4,0},{8,4},{12,8},{16,12},{20,16},{24,20},{28,24},{5,1},{9,5},{13... | collective-permute-start | bytes 786440 | tf_op jit(solution)/shard_map/ppermute | solution.py:271
Sparse Core Ops, SparseCore 0:
  10.1 58.6 all-gather.1
